TPU v7x, 256 devices: a whole 4x4x8 slice. The times are simulated.
256 devices in a mesh: inst: 64 (over z, y_lo, x), space: 4 (over y_hi, core).
Axes of the slice: x: 4, y: 4 (y_hi: 2, y_lo: 2; y = y_hi * 2 + y_lo), z: 8, core: 2. Of those that a mesh axis runs over, the one named last changes fastest.
Arguments:
- base_state: float32 [256, 5, 64, 512], P('inst', None, 'space'), may hold values from -3 to 3
- adjoint: float32 [256, 5, 64, 512], P('inst', None, 'space'), may hold values from -6 to 6
- gradient: float32 [256, 5, 64, 512], P('inst', None, 'space'), may hold values from -6 to 6
- cell_types: int32 [64, 512], P('space'), may hold values from 0 to 2
Outputs:
- adjoint_residual: float32 [256, 5, 64, 512], P('inst', None, 'space')
Inputs may be any that keep to these rules, and one draw needn't show every extreme that they name: `cell_types`: 0 marks plasma cells, 1 wall cells, 2 anode injection cells.
All inputs are finite; a program needn't handle non-finite values.
Results may differ from a plain program's by a relative error of at most 0.00005.
Values sent between devices are 32-bit elements; how exact they have to be, the bound alone decides.
No kernel may reach another device: no remote copies, remote signals or barrier semaphores. Data moves between devices by JAX's collectives and lax.ppermute only.
A program may use at most 64 MiB of HBM per device.

v0:
```python
import math

import jax
import jax.numpy as jnp
from jax import lax
from jax.sharding import PartitionSpec as P

dissipation = 0.5
ionize_rate = 0.6
collide_rate = 0.4
energy_loss = 0.3
field_push = 0.8
wall_relax = 2.0
time_factor = 4.0


def extended_2(block, sides, width):
    for axis, dim in sides:
        count = lax.axis_size(axis)
        forward = [(i, i + 1) for i in range(count - 1)]
        backward = [(target, source) for source, target in forward]
        low = lax.ppermute(
            lax.slice_in_dim(block, block.shape[dim] - width, None, axis=dim), axis, forward
        )
        high = lax.ppermute(lax.slice_in_dim(block, 0, width, axis=dim), axis, backward)
        block = jnp.concatenate([low, block, high], axis=dim)
    return block


def from_partner(x, axis, distance):
    return lax.ppermute(x, axis, [(i, i ^ 1 << distance) for i in range(lax.axis_size(axis))])


def axial_flux(state):
    ion_log, axial_vel, radial_vel, neutral_log, temper = (
        state[0],
        state[1],
        state[2],
        state[3],
        state[4],
    )
    return jnp.stack(
        [
            jnp.exp(ion_log) * axial_vel,
            0.5 * axial_vel * axial_vel + temper,
            axial_vel * radial_vel,
            jnp.exp(neutral_log),
            axial_vel * temper,
        ],
        axis=0,
    )


def radial_flux(state):
    ion_log, axial_vel, radial_vel, neutral_log, temper = (
        state[0],
        state[1],
        state[2],
        state[3],
        state[4],
    )
    return jnp.stack(
        [
            jnp.exp(ion_log) * radial_vel,
            axial_vel * radial_vel,
            0.5 * radial_vel * radial_vel + temper,
            0.5 * jnp.exp(neutral_log) * radial_vel,
            radial_vel * temper,
        ],
        axis=0,
    )


def source_terms(state):
    axial_vel, radial_vel, neutral_log, temper = (state[1], state[2], state[3], state[4])
    ionize = ionize_rate * jnp.exp(neutral_log) * temper
    return jnp.stack(
        [
            ionize,
            field_push * temper - collide_rate * axial_vel,
            -collide_rate * radial_vel,
            -ionize,
            field_push * axial_vel - energy_loss * temper * temper,
        ],
        axis=0,
    )


def numeric_flux(flux, left, right):
    return 0.5 * (flux(left) + flux(right)) - dissipation * (right - left)


def spatial_pieces(extended):
    inner = extended[:, 1:-1]
    axial_faces = numeric_flux(axial_flux, extended[:, :-1], extended[:, 1:])
    padded = jnp.pad(inner, ((0, 0), (0, 0), (1, 1)))
    radial_faces = numeric_flux(radial_flux, padded[:, :, :-1], padded[:, :, 1:])
    radial_div = radial_faces[:, :, :-1] - radial_faces[:, :, 1:]
    return (axial_faces, radial_div, source_terms(inner))


def spatial_adjoint(extended, weighted, source_side):
    _, pullback = jax.vjp(spatial_pieces, extended)
    axial_side = weighted[:, 1:] - weighted[:, :-1]
    (cotangent,) = pullback((axial_side, weighted[:, 1:-1], source_side))
    return cotangent[:, 1:-1]


def rotate(pair, angle):
    cosine = jnp.cos(angle)
    sine = jnp.sin(angle)
    return jnp.stack([pair[0] * cosine - pair[1] * sine, pair[0] * sine + pair[1] * cosine], axis=0)


def per_device(base_state, adjoint, gradient, cell_types):
    fluid = (cell_types != 1).astype(jnp.float32)
    feed = (cell_types == 0).astype(jnp.float32) + 3.0 * (cell_types == 2).astype(jnp.float32)
    wall = (cell_types == 1).astype(jnp.float32)
    local = adjoint.shape[0]
    fields = adjoint.shape[1]
    devices = lax.axis_size("inst")
    index = lax.axis_index("inst")
    total = local * devices
    device_bits = devices.bit_length() - 1
    local_bits = local.bit_length() - 1
    positions = jnp.arange(local, dtype=jnp.int32)
    stacked = jnp.concatenate([base_state, fluid * adjoint], axis=1)
    extended = extended_2(stacked, (("space", 2),), 1)
    spatial = jax.vmap(spatial_adjoint)(extended[:, :fields], extended[:, fields:], feed * adjoint)

    def section_info(bit):
        half = local * 2**bit
        lower = index >> bit & 1 == 0
        offset = index % 2**bit * local + positions
        angle = 2.0 * math.pi / (2 * half) * offset.astype(jnp.float32)
        return (lower, angle.reshape(local, 1, 1, 1))

    top_bit = device_bits - 1
    lower, angle = section_info(top_bit)
    partner = from_partner(adjoint, "inst", top_bit)
    merged = jnp.where(lower, adjoint + partner, partner - adjoint)
    turned = jnp.where(lower, 0.0, angle)
    spectra = jnp.stack([merged * jnp.cos(turned), -merged * jnp.sin(turned)], axis=0)
    for bit in range(top_bit - 1, -1, -1):
        lower, angle = section_info(bit)
        partner = from_partner(spectra, "inst", bit)
        merged = jnp.where(lower, spectra + partner, partner - spectra)
        spectra = rotate(merged, jnp.where(lower, 0.0, -angle))
    trailing = spectra.shape[2:]
    for level in range(local_bits):
        half = local >> level + 1
        shaped = spectra.reshape((2, local // (2 * half), 2, half) + trailing)
        first = shaped[:, :, 0]
        second = shaped[:, :, 1]
        angle = (2.0 * math.pi / (2 * half) * jnp.arange(half, dtype=jnp.float32)).reshape(
            half, 1, 1, 1
        )
        spectra = jnp.stack([first + second, rotate(first - second, -angle)], axis=2).reshape(
            spectra.shape
        )
    total_bits = device_bits + local_bits
    place = index * local + positions
    freq = jnp.zeros((local,), jnp.int32)
    for bit in range(total_bits):
        freq = freq + ((place >> bit & 1) << total_bits - 1 - bit)
    wave = jnp.where(freq < total // 2, freq, freq - total)
    wave = jnp.where(freq == total // 2, 0, wave)
    factor = (-time_factor / (total * total) * wave.astype(jnp.float32)).reshape(local, 1, 1, 1)
    spectra = jnp.stack([-factor * spectra[1], factor * spectra[0]], axis=0)
    for level in range(local_bits):
        half = 1 << level
        shaped = spectra.reshape((2, local // (2 * half), 2, half) + trailing)
        first = shaped[:, :, 0]
        angle = (2.0 * math.pi / (2 * half) * jnp.arange(half, dtype=jnp.float32)).reshape(
            half, 1, 1, 1
        )
        second = rotate(shaped[:, :, 1], angle)
        spectra = jnp.stack([first + second, first - second], axis=2).reshape(spectra.shape)
    for bit in range(0, top_bit):
        lower, angle = section_info(bit)
        partner = from_partner(spectra, "inst", bit)
        turned = rotate(jnp.where(lower, partner, spectra), angle)
        kept = jnp.where(lower, spectra, partner)
        spectra = jnp.where(lower, kept + turned, kept - turned)
    lower, angle = section_info(top_bit)
    mine = jnp.where(lower, spectra[0], spectra[0] * jnp.cos(angle) - spectra[1] * jnp.sin(angle))
    partner = from_partner(mine, "inst", top_bit)
    time_term = jnp.where(lower, mine + partner, partner - mine)
    return time_term + spatial - wall_relax * wall * adjoint - gradient


def solution(mesh):
    return jax.shard_map(
        per_device,
        mesh=mesh,
        in_specs=(
            P("inst", None, "space", None),
            P("inst", None, "space", None),
            P("inst", None, "space", None),
            P("space", None),
        ),
        out_specs=P("inst", None, "space", None),
        check_vma=False,
    )
```

profile of v0, /device:TPU:16, one launch (start us, length us, event | category | flops | bytes accessed | tf_op | source)
XLA Modules:
  0.0 427.2 jit_solution(10183852156662275002)
XLA Ops:
  0.0 7.2 %collective-permute-start = (f32[4,5,16,512]{3,2,1,0:T(8,128)}, f32[4,5,16,512]{3,2,1,0:T(8,128)S(1)}, u32[]{:S(2)}, u32[]{:S(2)}) collective-permute-start(f32[4,5,16,512]{3,2,1,0:T(8,128)} %param.5), channel_id=1, source_target_pairs={{0,128},{4,132},{8,136},{12,140},{16,144},{20,148},{24,152},{28,15... | collective-permute-start | bytes 1966088 | tf_op jit(solution)/shard_map/ppermute | solution.py:31
  8.8 16.8 %collective-permute-done = f32[4,5,16,512]{3,2,1,0:T(8,128)S(1)} collective-permute-done((f32[4,5,16,512]{3,2,1,0:T(8,128)}, f32[4,5,16,512]{3,2,1,0:T(8,128)S(1)}, u32[]{:S(2)}, u32[]{:S(2)}) %collective-permute-start) | collective-permute-done | bytes 655392 | tf_op jit(solution)/shard_map/ppermute | solution.py:31
  26.4 1.8 multiply_bitcast_fusion.1
  29.4 12.5 %collective-permute-start.1 = (f32[2,4,5,16,512]{4,3,2,1,0:T(8,128)}, f32[2,4,5,16,512]{4,3,2,1,0:T(8,128)}, u32[]{:S(2)}, u32[]{:S(2)}) collective-permute-start(f32[2,4,5,16,512]{4,3,2,1,0:T(8,128)} %pad_maximum_fusion.1), channel_id=1, source_target_pairs={{0,64},{4,68},{8,72},{12,76},{16,80},{20,84},{24,88},{28,92},{32,9... | collective-permute-start | bytes 3932168 | tf_op jit(solution)/shard_map/ppermute | solution.py:31
  42.0 56.5 %collective-permute-done.1 = f32[2,4,5,16,512]{4,3,2,1,0:T(8,128)} collective-permute-done((f32[2,4,5,16,512]{4,3,2,1,0:T(8,128)}, f32[2,4,5,16,512]{4,3,2,1,0:T(8,128)}, u32[]{:S(2)}, u32[]{:S(2)}) %collective-permute-start.1) | collective-permute-done | bytes 1310752 | tf_op jit(solution)/shard_map/ppermute | solution.py:31
  98.5 1.6 subtract_select_fusion.9
  101.6 29.7 %collective-permute-done.2 = f32[2,4,5,16,512]{4,3,2,1,0:T(8,128)} collective-permute-done((f32[2,4,5,16,512]{4,3,2,1,0:T(8,128)}, f32[2,4,5,16,512]{4,3,2,1,0:T(8,128)}, u32[]{:S(2)}, u32[]{:S(2)}) %collective-permute-start.2) | collective-permute-done | bytes 1310752 | tf_op jit(solution)/shard_map/ppermute | solution.py:31
  131.3 1.6 subtract_select_fusion.8
  134.4 1.3 collective-permute-start.3
  135.7 27.5 %collective-permute-done.3 = f32[2,4,5,16,512]{4,3,2,1,0:T(8,128)} collective-permute-done((f32[2,4,5,16,512]{4,3,2,1,0:T(8,128)}, f32[2,4,5,16,512]{4,3,2,1,0:T(8,128)}, u32[]{:S(2)}, u32[]{:S(2)}) %collective-permute-start.3) | collective-permute-done | bytes 1310752 | tf_op jit(solution)/shard_map/ppermute | solution.py:31
  163.2 1.6 subtract_select_fusion.7
  166.3 3.0 collective-permute-start.4
  169.3 26.3 %collective-permute-done.4 = f32[2,4,5,16,512]{4,3,2,1,0:T(8,128)} collective-permute-done((f32[2,4,5,16,512]{4,3,2,1,0:T(8,128)}, f32[2,4,5,16,512]{4,3,2,1,0:T(8,128)}, u32[]{:S(2)}, u32[]{:S(2)}) %collective-permute-start.4) | collective-permute-done | bytes 1310752 | tf_op jit(solution)/shard_map/ppermute | solution.py:31
  195.6 1.6 subtract_select_fusion.6
  198.7 1.5 collective-permute-start.5
  200.4 25.3 %collective-permute-done.5 = f32[2,4,5,16,512]{4,3,2,1,0:T(8,128)} collective-permute-done((f32[2,4,5,16,512]{4,3,2,1,0:T(8,128)}, f32[2,4,5,16,512]{4,3,2,1,0:T(8,128)}, u32[]{:S(2)}, u32[]{:S(2)}) %collective-permute-start.5) | collective-permute-done | bytes 1310752 | tf_op jit(solution)/shard_map/ppermute | solution.py:31
  225.7 1.6 subtract_select_fusion.5
  230.2 1.6 collective-permute-start.6
  231.8 24.4 %collective-permute-done.6 = f32[2,4,5,16,512]{4,3,2,1,0:T(8,128)S(1)} collective-permute-done((f32[2,4,5,16,512]{4,3,2,1,0:T(8,128)S(1)}, f32[2,4,5,16,512]{4,3,2,1,0:T(8,128)S(1)}, u32[]{:S(2)}, u32[]{:S(2)}) %collective-permute-start.6) | collective-permute-done | bytes 1310752 | tf_op jit(solution)/shard_map/ppermute | solution.py:31
  257.6 4.1 collective-permute-start.7
  261.7 24.6 %collective-permute-done.7 = f32[2,4,5,16,512]{4,3,2,1,0:T(8,128)S(1)} collective-permute-done((f32[2,4,5,16,512]{4,3,2,1,0:T(8,128)S(1)}, f32[2,4,5,16,512]{4,3,2,1,0:T(8,128)S(1)}, u32[]{:S(2)}, u32[]{:S(2)}) %collective-permute-start.7) | collective-permute-done | bytes 1310752 | tf_op jit(solution)/shard_map/ppermute | solution.py:31
  287.4 1.6 collective-permute-start.8
  289.0 24.4 %collective-permute-done.8 = f32[2,4,5,16,512]{4,3,2,1,0:T(8,128)S(1)} collective-permute-done((f32[2,4,5,16,512]{4,3,2,1,0:T(8,128)S(1)}, f32[2,4,5,16,512]{4,3,2,1,0:T(8,128)S(1)}, u32[]{:S(2)}, u32[]{:S(2)}) %collective-permute-start.8) | collective-permute-done | bytes 1310752 | tf_op jit(solution)/shard_map/ppermute | solution.py:31
  314.7 1.8 collective-permute-start.9
  317.5 25.8 %collective-permute-done.9 = f32[2,4,5,16,512]{4,3,2,1,0:T(8,128)S(1)} collective-permute-done((f32[2,4,5,16,512]{4,3,2,1,0:T(8,128)S(1)}, f32[2,4,5,16,512]{4,3,2,1,0:T(8,128)S(1)}, u32[]{:S(2)}, u32[]{:S(2)}) %collective-permute-start.9) | collective-permute-done | bytes 1310752 | tf_op jit(solution)/shard_map/ppermute | solution.py:31
  344.6 1.9 collective-permute-start.12
  346.6 2.4 collective-permute-start.13
  349.8 4.5 %collective-permute-done.13 = f32[4,10,1,512]{3,1,2,0:T(8,128)S(1)} collective-permute-done((f32[4,10,1,512]{3,1,2,0:T(8,128)S(1)}, f32[4,10,1,512]{3,1,2,0:T(8,128)S(1)}, u32[]{:S(2)}, u32[]{:S(2)}) %collective-permute-start.13) | collective-permute-done | bytes 81952 | tf_op jit(solution)/shard_map/ppermute | solution.py:22
  355.3 38.7 %collective-permute-done.10 = f32[2,4,5,16,512]{4,3,2,1,0:T(8,128)S(1)} collective-permute-done((f32[2,4,5,16,512]{4,3,2,1,0:T(8,128)S(1)}, f32[2,4,5,16,512]{4,3,2,1,0:T(8,128)S(1)}, u32[]{:S(2)}, u32[]{:S(2)}) %collective-permute-start.10) | collective-permute-done | bytes 1310752 | tf_op jit(solution)/shard_map/ppermute | solution.py:31
  395.2 1.8 collective-permute-start.11
  397.9 27.8 %collective-permute-done.11 = f32[4,5,16,512]{3,2,1,0:T(8,128)S(1)} collective-permute-done((f32[4,5,16,512]{3,2,1,0:T(8,128)S(1)}, f32[4,5,16,512]{3,2,1,0:T(8,128)S(1)}, u32[]{:S(2)}, u32[]{:S(2)}) %collective-permute-start.11) | collective-permute-done | bytes 655392 | tf_op jit(solution)/shard_map/ppermute | solution.py:31
  425.7 1.6 fusion.5
  (88 shorter events, 22.6 us)
Async XLA Ops:
  0.0 25.6 %collective-permute-start = (f32[4,5,16,512]{3,2,1,0:T(8,128)}, f32[4,5,16,512]{3,2,1,0:T(8,128)S(1)}, u32[]{:S(2)}, u32[]{:S(2)}) collective-permute-start(f32[4,5,16,512]{3,2,1,0:T(8,128)} %param.5), channel_id=1, source_target_pairs={{0,128},{4,132},{8,136},{12,140},{16,144},{20,148},{24,152},{28,15... | collective-permute-start | bytes 1966088 | tf_op jit(solution)/shard_map/ppermute | solution.py:31
  25.6 0.8 copy-start.3
  29.4 69.1 %collective-permute-start.1 = (f32[2,4,5,16,512]{4,3,2,1,0:T(8,128)}, f32[2,4,5,16,512]{4,3,2,1,0:T(8,128)}, u32[]{:S(2)}, u32[]{:S(2)}) collective-permute-start(f32[2,4,5,16,512]{4,3,2,1,0:T(8,128)} %pad_maximum_fusion.1), channel_id=1, source_target_pairs={{0,64},{4,68},{8,72},{12,76},{16,80},{20,84},{24,88},{28,92},{32,9... | collective-permute-start | bytes 3932168 | tf_op jit(solution)/shard_map/ppermute | solution.py:31
  101.6 29.7 %collective-permute-start.2 = (f32[2,4,5,16,512]{4,3,2,1,0:T(8,128)}, f32[2,4,5,16,512]{4,3,2,1,0:T(8,128)}, u32[]{:S(2)}, u32[]{:S(2)}) collective-permute-start(f32[2,4,5,16,512]{4,3,2,1,0:T(8,128)} %pad_maximum_fusion.2), channel_id=1, source_target_pairs={{0,32},{4,36},{8,40},{12,44},{16,48},{20,52},{24,56},{28,60},{32,0... | collective-permute-start | bytes 3932168 | tf_op jit(solution)/shard_map/ppermute | solution.py:31
  134.4 28.8 %collective-permute-start.3 = (f32[2,4,5,16,512]{4,3,2,1,0:T(8,128)}, f32[2,4,5,16,512]{4,3,2,1,0:T(8,128)}, u32[]{:S(2)}, u32[]{:S(2)}) collective-permute-start(f32[2,4,5,16,512]{4,3,2,1,0:T(8,128)} %pad_maximum_fusion.3), channel_id=1, source_target_pairs={{0,16},{4,20},{8,24},{12,28},{16,0},{20,4},{24,8},{28,12},{32,48},... | collective-permute-start | bytes 3932168 | tf_op jit(solution)/shard_map/ppermute | solution.py:31
  166.3 29.4 %collective-permute-start.4 = (f32[2,4,5,16,512]{4,3,2,1,0:T(8,128)}, f32[2,4,5,16,512]{4,3,2,1,0:T(8,128)}, u32[]{:S(2)}, u32[]{:S(2)}) collective-permute-start(f32[2,4,5,16,512]{4,3,2,1,0:T(8,128)} %pad_maximum_fusion.4), channel_id=1, source_target_pairs={{0,8},{4,12},{8,0},{12,4},{16,24},{20,28},{24,16},{28,20},{32,40},... | collective-permute-start | bytes 3932168 | tf_op jit(solution)/shard_map/ppermute | solution.py:31
  198.7 26.9 %collective-permute-start.5 = (f32[2,4,5,16,512]{4,3,2,1,0:T(8,128)}, f32[2,4,5,16,512]{4,3,2,1,0:T(8,128)}, u32[]{:S(2)}, u32[]{:S(2)}) collective-permute-start(f32[2,4,5,16,512]{4,3,2,1,0:T(8,128)} %pad_maximum_fusion.5), channel_id=1, source_target_pairs={{0,4},{4,0},{8,12},{12,8},{16,20},{20,16},{24,28},{28,24},{32,36},... | collective-permute-start | bytes 3932168 | tf_op jit(solution)/shard_map/ppermute | solution.py:31
  230.2 26.1 %collective-permute-start.6 = (f32[2,4,5,16,512]{4,3,2,1,0:T(8,128)S(1)}, f32[2,4,5,16,512]{4,3,2,1,0:T(8,128)S(1)}, u32[]{:S(2)}, u32[]{:S(2)}) collective-permute-start(f32[2,4,5,16,512]{4,3,2,1,0:T(8,128)S(1)} %bitcast.63), channel_id=1, source_target_pairs={{0,4},{4,0},{8,12},{12,8},{16,20},{20,16},{24,28},{28,24},{32,36},... | collective-permute-start | bytes 3932168 | tf_op jit(solution)/shard_map/ppermute | solution.py:31
  257.6 28.7 %collective-permute-start.7 = (f32[2,4,5,16,512]{4,3,2,1,0:T(8,128)S(1)}, f32[2,4,5,16,512]{4,3,2,1,0:T(8,128)S(1)}, u32[]{:S(2)}, u32[]{:S(2)}) collective-permute-start(f32[2,4,5,16,512]{4,3,2,1,0:T(8,128)S(1)} %subtract_select_fusion.4), channel_id=1, source_target_pairs={{0,8},{4,12},{8,0},{12,4},{16,24},{20,28},{24,16},{28,20},{32,40},... | collective-permute-start | bytes 3932168 | tf_op jit(solution)/shard_map/ppermute | solution.py:31
  287.4 26.0 %collective-permute-start.8 = (f32[2,4,5,16,512]{4,3,2,1,0:T(8,128)S(1)}, f32[2,4,5,16,512]{4,3,2,1,0:T(8,128)S(1)}, u32[]{:S(2)}, u32[]{:S(2)}) collective-permute-start(f32[2,4,5,16,512]{4,3,2,1,0:T(8,128)S(1)} %subtract_select_fusion.3), channel_id=1, source_target_pairs={{0,16},{4,20},{8,24},{12,28},{16,0},{20,4},{24,8},{28,12},{32,48},... | collective-permute-start | bytes 3932168 | tf_op jit(solution)/shard_map/ppermute | solution.py:31
  314.7 2.2 copy-start
  314.7 28.6 %collective-permute-start.9 = (f32[2,4,5,16,512]{4,3,2,1,0:T(8,128)S(1)}, f32[2,4,5,16,512]{4,3,2,1,0:T(8,128)S(1)}, u32[]{:S(2)}, u32[]{:S(2)}) collective-permute-start(f32[2,4,5,16,512]{4,3,2,1,0:T(8,128)S(1)} %subtract_select_fusion.2), channel_id=1, source_target_pairs={{0,32},{4,36},{8,40},{12,44},{16,48},{20,52},{24,56},{28,60},{32,0... | collective-permute-start | bytes 3932168 | tf_op jit(solution)/shard_map/ppermute | solution.py:31
  344.3 49.7 %collective-permute-start.10 = (f32[2,4,5,16,512]{4,3,2,1,0:T(8,128)S(1)}, f32[2,4,5,16,512]{4,3,2,1,0:T(8,128)S(1)}, u32[]{:S(2)}, u32[]{:S(2)}) collective-permute-start(f32[2,4,5,16,512]{4,3,2,1,0:T(8,128)S(1)} %subtract_select_fusion.1), channel_id=1, source_target_pairs={{0,64},{4,68},{8,72},{12,76},{16,80},{20,84},{24,88},{28,92},{32,9... | collective-permute-start | bytes 3932168 | tf_op jit(solution)/shard_map/ppermute | solution.py:31
  344.6 5.1 %collective-permute-start.12 = (f32[4,10,1,512]{3,1,2,0:T(8,128)S(1)}, f32[4,10,1,512]{3,1,2,0:T(8,128)S(1)}, u32[]{:S(2)}, u32[]{:S(2)}) collective-permute-start(f32[4,10,1,512]{3,1,2,0:T(8,128)S(1)} %copy.33), channel_id=1, source_target_pairs={{1,0},{2,1},{3,2},{5,4},{6,5},{7,6},{9,8},{10,9},{11,10},{13,12},{... | collective-permute-start | bytes 245768 | tf_op jit(solution)/shard_map/ppermute | solution.py:25
  346.6 7.8 %collective-permute-start.13 = (f32[4,10,1,512]{3,1,2,0:T(8,128)S(1)}, f32[4,10,1,512]{3,1,2,0:T(8,128)S(1)}, u32[]{:S(2)}, u32[]{:S(2)}) collective-permute-start(f32[4,10,1,512]{3,1,2,0:T(8,128)S(1)} %copy.35), channel_id=1, source_target_pairs={{0,1},{1,2},{2,3},{4,5},{5,6},{6,7},{8,9},{9,10},{10,11},{12,13},{... | collective-permute-start | bytes 245768 | tf_op jit(solution)/shard_map/ppermute | solution.py:22
  395.2 30.4 %collective-permute-start.11 = (f32[4,5,16,512]{3,2,1,0:T(8,128)S(1)}, f32[4,5,16,512]{3,2,1,0:T(8,128)S(1)}, u32[]{:S(2)}, u32[]{:S(2)}) collective-permute-start(f32[4,5,16,512]{3,2,1,0:T(8,128)S(1)} %fusion.9), channel_id=1, source_target_pairs={{0,128},{4,132},{8,136},{12,140},{16,144},{20,148},{24,152},{28,15... | collective-permute-start | bytes 1966088 | tf_op jit(solution)/shard_map/ppermute | solution.py:31
  397.4 28.3 %copy-start.1 = (f32[4,5,16,512]{3,2,1,0:T(8,128)S(1)}, f32[4,5,16,512]{3,2,1,0:T(8,128)}, u32[]{:S(2)}) copy-start(f32[4,5,16,512]{3,2,1,0:T(8,128)} %param.5) | copy-start | bytes 1966084
  397.4 28.3 %copy-start.2 = (f32[4,5,16,512]{3,2,1,0:T(8,128)S(1)}, f32[4,5,16,512]{3,2,1,0:T(8,128)}, u32[]{:S(2)}) copy-start(f32[4,5,16,512]{3,2,1,0:T(8,128)} %param.6) | copy-start | bytes 1966084
where the time goes:
time: 428 us; the launch traced here: 427 us
  waiting for transfers between devices  352 us (82%)
  starting transfers between devices  40.7 us (10%)
  other arithmetic  32.7 us (8%)
    ppermute x12, waiting for transfers between devices, from_partner(): lax.ppermute(x, axis, [(i, i ^ 1 << distance) for i in range(lax.axis_siz...  348 us
    ppermute x12, starting transfers between devices, from_partner(): lax.ppermute(x, axis, [(i, i ^ 1 << distance) for i in range(lax.axis_siz...  36.4 us
  transfers between devices with their start and end apart: 14, of which 13 were waited for; matrix products, arithmetic and copies ran while one was open for 1% of the time, Pallas kernels for 0%

commit v1 on v0

v1 whole, which is shorter than its diff:
```python
import jax
import jax.numpy as jnp
import numpy as np
from jax import lax
from jax.experimental import pallas as pl
from jax.experimental.pallas import tpu as pltpu
from jax.sharding import PartitionSpec as P

dissipation = 0.5
ionize_rate = 0.6
collide_rate = 0.4
energy_loss = 0.3
field_push = 0.8
wall_relax = 2.0
time_factor = 4.0

LANES = 128
SUB = 8


def derivative_matrix(total):
    gap = np.arange(total)[:, None] - np.arange(total)[None, :]
    off = gap != 0
    angle = np.where(off, np.pi * gap / total, 1.0)
    entry = np.where(off, 0.5 * np.where(gap % 2 == 0, 1.0, -1.0) / np.tan(angle), 0.0)
    entry = -(time_factor / total) * entry
    high = entry.astype(jnp.bfloat16)
    low = (entry - high.astype(np.float64)).astype(jnp.bfloat16)
    return np.concatenate([high, high, low], axis=1)


def pack_kernel(chunk, parts, x_ref, o_ref):
    for d in range(parts):
        o_ref[pl.ds(d * chunk, chunk), :] = x_ref[pl.ds(d, chunk, stride=parts), :]


def edge_kernel(x_ref, c_ref, low_ref, high_ref):
    local, fields, axial, _ = x_ref.shape
    for row, o_ref in ((0, low_ref), (axial - 1, high_ref)):
        fluid = (c_ref[row : row + 1, :] != 1).astype(jnp.float32)
        for i in range(local):
            for f in range(fields):
                o_ref[i * fields + f] = fluid * x_ref[i, f, row : row + 1, :]


def spatial_kernel(state_ref, adjoint_ref, gradient_ref, cell_ref, before_ref, after_ref, o_ref):
    local, fields, axial, radial = state_ref.shape
    cell = cell_ref[...]
    fluid = (cell != 1).astype(jnp.float32)
    feed = (cell == 0).astype(jnp.float32) + 3.0 * (cell == 2).astype(jnp.float32)
    relax = wall_relax * (cell == 1).astype(jnp.float32)
    row = lax.broadcasted_iota(jnp.int32, (axial, radial), 0)
    lane = lax.broadcasted_iota(jnp.int32, (axial, radial), 1)
    for i in range(local):
        axial_diff, radial_diff, source, spread = [], [], [], []
        for f in range(fields):
            adjoint = adjoint_ref[i, f]
            weighted = fluid * adjoint
            before = jnp.where(row == 0, before_ref[i * fields + f], pltpu.roll(weighted, 1, 0))
            after = jnp.where(
                row == axial - 1, after_ref[i * fields + f], pltpu.roll(weighted, axial - 1, 0)
            )
            inward = jnp.where(lane == 0, 0.0, pltpu.roll(weighted, 1, 1))
            outward = jnp.where(lane == radial - 1, 0.0, pltpu.roll(weighted, radial - 1, 1))
            axial_diff.append(0.5 * (after - before))
            radial_diff.append(0.5 * (outward - inward))
            source.append(feed * adjoint)
            spread.append(
                dissipation * ((after + before) + (outward + inward))
                - (4.0 * dissipation) * weighted
                - relax * adjoint
                - gradient_ref[i, f]
            )
        ion = jnp.exp(state_ref[i, 0])
        u = state_ref[i, 1]
        v = state_ref[i, 2]
        neutral = jnp.exp(state_ref[i, 3])
        temper = state_ref[i, 4]
        p, q, m = axial_diff, radial_diff, source
        ionize = ionize_rate * neutral * (m[0] - m[3])
        o_ref[i, 0] = spread[0] + ion * (u * p[0] + v * q[0])
        o_ref[i, 1] = (
            spread[1]
            + (ion * p[0] + u * p[1] + v * (p[2] + q[1]) + temper * p[4])
            + (field_push * m[4] - collide_rate * m[1])
        )
        o_ref[i, 2] = (
            spread[2]
            + (ion * q[0] + u * (p[2] + q[1]) + v * q[2] + 0.5 * neutral * q[3] + temper * q[4])
            - collide_rate * m[2]
        )
        o_ref[i, 3] = spread[3] + neutral * (p[3] + 0.5 * v * q[3]) + ionize * temper
        o_ref[i, 4] = (
            spread[4]
            + (p[1] + q[2] + u * p[4] + v * q[4])
            + (ionize + field_push * m[1] - (2.0 * energy_loss) * temper * m[4])
        )


def product_kernel(fields, total, d_ref, x_ref, o_ref):
    columns = jnp.concatenate(
        [x_ref[pl.ds(f, total, stride=fields), :] for f in range(fields)], axis=1
    )
    high = columns.astype(jnp.bfloat16)
    low = (columns - high.astype(jnp.float32)).astype(jnp.bfloat16)
    stacked = jnp.concatenate([high, low, high], axis=0)
    result = jnp.dot(d_ref[...], stacked, preferred_element_type=jnp.float32)
    for f in range(fields):
        o_ref[pl.ds(f, total, stride=fields), :] = result[:, f * LANES : (f + 1) * LANES]


def combine_kernel(chunk, parts, t_ref, s_ref, o_ref):
    for q in range(chunk):
        rows = pl.ds(q * parts, parts)
        o_ref[rows, :] = t_ref[pl.ds(q, parts, stride=chunk), :] + s_ref[rows, :]


def to_tiles(x):
    local, fields, axial, radial = x.shape
    x = x.reshape(local, fields, axial // SUB, SUB, radial // LANES, LANES)
    return x.transpose(0, 1, 2, 4, 3, 5).reshape(-1, LANES)


def from_tiles(x, shape):
    local, fields, axial, radial = shape
    x = x.reshape(local, fields, axial // SUB, radial // LANES, SUB, LANES)
    return x.transpose(0, 1, 2, 4, 3, 5).reshape(shape)


def per_device(base_state, adjoint, gradient, cell_types):
    shape = adjoint.shape
    local, fields, _, radial = shape
    parts = lax.axis_size("inst")
    total = local * parts
    chunk = local * fields
    rows = adjoint.size // LANES
    space = pl.BlockSpec(memory_space=pltpu.VMEM)

    def run(kernel, name, outs, *operands, flops=0):
        single = isinstance(outs, tuple)
        shapes = [jax.ShapeDtypeStruct(s, jnp.float32) for s in ([outs] if single else outs)]
        moved = sum(x.size for x in operands) + sum(s.size for s in shapes)
        return pl.pallas_call(
            kernel,
            out_shape=shapes[0] if single else shapes,
            in_specs=[space] * len(operands),
            out_specs=space if single else [space] * len(shapes),
            name=name,
            cost_estimate=pl.CostEstimate(
                flops=flops, bytes_accessed=4 * moved, transcendentals=0
            ),
        )(*operands)

    def exchange(x):
        x = x.reshape(parts, fields, local, LANES)
        return lax.all_to_all(x, "inst", 0, 0).reshape(rows, LANES)

    flat = (rows, LANES)
    packed = run(lambda *r: pack_kernel(chunk, parts, *r), "pack", flat, to_tiles(adjoint))
    columns = exchange(packed)
    product = run(
        lambda *r: product_kernel(fields, total, *r),
        "time_product",
        flat,
        jnp.asarray(derivative_matrix(total)),
        columns,
        flops=6 * total * total * fields * LANES,
    )
    time_part = exchange(product)

    edge = (chunk, 1, radial)
    first, last = run(edge_kernel, "edges", [edge, edge], adjoint, cell_types)
    count = lax.axis_size("space")
    up = [(i, i + 1) for i in range(count - 1)]
    down = [(i + 1, i) for i in range(count - 1)]
    before = lax.ppermute(last, "space", up)
    after = lax.ppermute(first, "space", down)
    rest = run(
        spatial_kernel,
        "spatial",
        shape,
        base_state,
        adjoint,
        gradient,
        cell_types,
        before,
        after,
        flops=60 * adjoint.size,
    )
    out = run(
        lambda *r: combine_kernel(chunk, parts, *r), "combine", flat, time_part, to_tiles(rest)
    )
    return from_tiles(out, shape)


def solution(mesh):
    return jax.shard_map(
        per_device,
        mesh=mesh,
        in_specs=(
            P("inst", None, "space", None),
            P("inst", None, "space", None),
            P("inst", None, "space", None),
            P("space", None),
        ),
        out_specs=P("inst", None, "space", None),
        check_vma=False,
    )
```

time: 428 us -> 67.1 us (0.16)
  waiting for transfers between devices: 352 us -> 7.12 us
  blocking collectives: 0 us -> 33.2 us
  other arithmetic: 32.7 us -> 0 us
  starting transfers between devices: 40.7 us -> 12.9 us
  Pallas kernels: 0 us -> 11.9 us
    ppermute x14 -> x2, waiting for transfers between devices: 352 us -> 1.97 us  [the longest x1 1.62 us: per_device(): after = lax.ppermute(first, 'space', down)]
    ppermute x14 -> x2, starting transfers between devices: 40.7 us -> 7.05 us  [the longest x1 5.15 us: per_device(): after = lax.ppermute(first, 'space', down)]
    all_to_all x0 -> x1, blocking collectives: none -> 33.2 us  [exchange(): return lax.all_to_all(x, 'inst', 0, 0).reshape(rows, LANES)]
    select_n x16 -> x0, other arithmetic: 12.5 us -> none  [the longest x5 8.06 us: per_device(): merged = jnp.where(lower, spectra + partner, partner - spectra)]
    pallas_call x0 -> x5, Pallas kernels: none -> 11.9 us  [run(): pl.pallas_call(kernel, out_shape=shapes[0] if single else shapes, in_spec...]
    another operation x11 -> x0, other arithmetic: 8.37 us -> none  [the longest x4 4.82 us: rotate(): jnp.stack([pair[0] * cosine - pair[1] * sine, pair[0] * sine + pair[1] *...]
    all_to_all x0 -> x1, starting transfers between devices: none -> 5.86 us  [exchange(): return lax.all_to_all(x, 'inst', 0, 0).reshape(rows, LANES)]
    all_to_all x0 -> x1, waiting for transfers between devices: none -> 5.15 us  [exchange(): return lax.all_to_all(x, 'inst', 0, 0).reshape(rows, LANES)]
  transfers between devices with their start and end apart: 14 -> 3, of which waited for: 13 -> 3; matrix products, arithmetic and copies ran while one was open for 1% -> 0% of each run, Pallas kernels for 0% -> 7%
where the time goes in v1:
time: 67.1 us; the launch traced here: 66.7 us
  blocking collectives  33.2 us (49%)
  starting transfers between devices  12.9 us (19%)
  Pallas kernels  11.9 us (18%)
  waiting for transfers between devices  7.12 us (11%)
  local copies, waits for them, and re-layouts  1.46 us (2%)
    all_to_all x1, blocking collectives, exchange(): return lax.all_to_all(x, 'inst', 0, 0).reshape(rows, LANES)  33.2 us
    pallas_call x5, Pallas kernels, run(): pl.pallas_call(kernel, out_shape=shapes[0] if single else shapes, in_spec...  11.9 us
    all_to_all x1, starting transfers between devices, exchange(): return lax.all_to_all(x, 'inst', 0, 0).reshape(rows, LANES)  5.86 us
    all_to_all x1, waiting for transfers between devices, exchange(): return lax.all_to_all(x, 'inst', 0, 0).reshape(rows, LANES)  5.15 us
    ppermute x1, starting transfers between devices, per_device(): after = lax.ppermute(first, 'space', down)  5.15 us
    ppermute x1, starting transfers between devices, per_device(): before = lax.ppermute(last, 'space', up)  1.91 us
    ppermute x1, waiting for transfers between devices, per_device(): after = lax.ppermute(first, 'space', down)  1.62 us
    unnamed x6, local copies, waits for them, and re-layouts  1.46 us
  transfers between devices with their start and end apart: 3, of which 3 were waited for; matrix products, arithmetic and copies ran while one was open for 0% of the time, Pallas kernels for 7%

profile of v1, /device:TPU:16, one launch (start us, length us, event | category | flops | bytes accessed | tf_op | source)
XLA Modules:
  0.0 66.7 jit_solution(3937940031232286421)
XLA Ops:
  0.0 2.3 %pack.1 = f32[1280,128]{1,0:T(8,128)} custom-call(f32[1280,128]{1,0:T(8,128)} %bitcast.19), custom_call_target="tpu_custom_call" | custom-call | bytes 1310720 | tf_op jit(solution)/shard_map/pack/pallas_call | solution.py:143
  2.3 33.2 %all_to_all.10 = f32[64,5,4,128]{3,2,1,0:T(4,128)} all-to-all(f32[64,5,4,128]{3,2,1,0:T(4,128)} %bitcast.22), channel_id=1, replica_groups=mesh['inst'=64,'space'=4] {'inst'}, dimensions={0} | all-to-all | bytes 1310720 | tf_op jit(solution)/shard_map/all_to_all | solution.py:156
  35.6 2.5 %time_product.1 = f32[1280,128]{1,0:T(8,128)} custom-call(bf16[256,768]{1,0:T(8,128)(2,1)} %constant.2.clone.r_0_, f32[1280,128]{1,0:T(8,128)} %bitcast.21), custom_call_target="tpu_custom_call" | custom-call | flops 251658240 | bytes 2097152 | tf_op jit(solution)/shard_map/time_product/pallas_call | solution.py:143
  38.1 5.9 %all-to-all-start.1 = ((f32[64,5,4,128]{3,2,1,0:T(4,128)}), f32[64,5,4,128]{3,2,1,0:T(4,128)S(1)}, u32[]{:S(2)}, u32[]{:S(2)}) async-start(f32[64,5,4,128]{3,2,1,0:T(4,128)} %bitcast.20), calls=%async_computation.1 | async-start | bytes 1310720 | tf_op jit(solution)/shard_map/all_to_all | solution.py:156
  43.9 1.7 %edges.1 = (f32[20,1,512]{2,1,0:T(1,128)}, f32[20,1,512]{2,1,0:T(1,128)}) custom-call(f32[4,5,16,512]{3,2,1,0:T(8,128)} %adjoint_ref.1, s32[16,512]{1,0:T(8,128)} %cell_ref.1), custom_call_target="tpu_custom_call" | custom-call | bytes 770048 | tf_op jit(solution)/shard_map/edges/pallas_call | solution.py:143
  45.7 1.9 %collective-permute-start = (f32[20,1,512]{2,1,0:T(1,128)}, f32[20,1,512]{2,1,0:T(1,128)S(1)}, u32[]{:S(2)}, u32[]{:S(2)}) collective-permute-start(f32[20,1,512]{2,1,0:T(1,128)} %get-tuple-element.7), channel_id=1, source_target_pairs={{0,1},{1,2},{2,3},{4,5},{5,6},{6,7},{8,9},{9,10},{10,11},{12,13},{... | collective-permute-start | bytes 122888 | tf_op jit(solution)/shard_map/ppermute | solution.py:176
  47.6 5.1 %collective-permute-start.1 = (f32[20,1,512]{2,1,0:T(1,128)}, f32[20,1,512]{2,1,0:T(1,128)S(1)}, u32[]{:S(2)}, u32[]{:S(2)}) collective-permute-start(f32[20,1,512]{2,1,0:T(1,128)} %get-tuple-element.8), channel_id=1, source_target_pairs={{1,0},{2,1},{3,2},{5,4},{6,5},{7,6},{9,8},{10,9},{11,10},{13,12},{... | collective-permute-start | bytes 122888 | tf_op jit(solution)/shard_map/ppermute | solution.py:177
  52.8 0.3 collective-permute-done.before_ref
  53.1 0.0 copy-start.1
  53.1 1.6 %collective-permute-done.1.after_ref = f32[20,1,512]{2,1,0:T(1,128)S(1)} collective-permute-done((f32[20,1,512]{2,1,0:T(1,128)}, f32[20,1,512]{2,1,0:T(1,128)S(1)}, u32[]{:S(2)}, u32[]{:S(2)}) %collective-permute-start.1) | collective-permute-done | bytes 40992 | tf_op jit(solution)/shard_map/ppermute | solution.py:177
  54.7 0.0 copy-done.1
  54.7 0.0 copy-start.2
  54.7 0.6 copy-done.2
  55.3 3.1 %spatial.1 = f32[4,5,16,512]{3,2,1,0:T(8,128)} custom-call(f32[4,5,16,512]{3,2,1,0:T(8,128)} %state_ref.1, f32[4,5,16,512]{3,2,1,0:T(8,128)} %adjoint_ref.1, f32[4,5,16,512]{3,2,1,0:T(8,128)} %gradient_ref.1, s32[16,512]{1,0:T(8,128)} %cell_ref.1, f32[20,1,512]{2,1,0:T(1,128)} %copy-done.1, f32[20,1,512]{2,1,0:T(1,128)} %copy-done.2), custom_call_target="tpu_custom_call" | custom-call | flops 9830400 | bytes 2736128 | tf_op jit(solution)/shard_map/spatial/pallas_call | solution.py:143
  58.5 5.2 %all-to-all-done.1 = f32[64,5,4,128]{3,2,1,0:T(4,128)S(1)} async-done(((f32[64,5,4,128]{3,2,1,0:T(4,128)}), f32[64,5,4,128]{3,2,1,0:T(4,128)S(1)}, u32[]{:S(2)}, u32[]{:S(2)}) %all-to-all-start.1) | async-done | bytes 655392 | tf_op jit(solution)/shard_map/all_to_all | solution.py:156
  63.6 0.0 copy-start
  63.6 0.8 %copy-done = f32[64,5,4,128]{3,2,1,0:T(4,128)} copy-done((f32[64,5,4,128]{3,2,1,0:T(4,128)}, f32[64,5,4,128]{3,2,1,0:T(4,128)S(1)}, u32[]{:S(2)}) %copy-start) | copy-done | bytes 655384
  64.5 2.2 %combine.1 = f32[1280,128]{1,0:T(8,128)} custom-call(f32[1280,128]{1,0:T(8,128)} %bitcast.23, f32[1280,128]{1,0:T(8,128)} %bitcast.24), custom_call_target="tpu_custom_call" | custom-call | bytes 1966080 | tf_op jit(solution)/shard_map/combine/pallas_call | solution.py:143
Async XLA Ops:
  38.1 25.6 %all-to-all-start.1 = ((f32[64,5,4,128]{3,2,1,0:T(4,128)}), f32[64,5,4,128]{3,2,1,0:T(4,128)S(1)}, u32[]{:S(2)}, u32[]{:S(2)}) async-start(f32[64,5,4,128]{3,2,1,0:T(4,128)} %bitcast.20), calls=%async_computation.1 | async-start | bytes 1310720 | tf_op jit(solution)/shard_map/all_to_all | solution.py:156
  45.7 7.4 %collective-permute-start = (f32[20,1,512]{2,1,0:T(1,128)}, f32[20,1,512]{2,1,0:T(1,128)S(1)}, u32[]{:S(2)}, u32[]{:S(2)}) collective-permute-start(f32[20,1,512]{2,1,0:T(1,128)} %get-tuple-element.7), channel_id=1, source_target_pairs={{0,1},{1,2},{2,3},{4,5},{5,6},{6,7},{8,9},{9,10},{10,11},{12,13},{... | collective-permute-start | bytes 122888 | tf_op jit(solution)/shard_map/ppermute | solution.py:176
  47.6 7.1 %collective-permute-start.1 = (f32[20,1,512]{2,1,0:T(1,128)}, f32[20,1,512]{2,1,0:T(1,128)S(1)}, u32[]{:S(2)}, u32[]{:S(2)}) collective-permute-start(f32[20,1,512]{2,1,0:T(1,128)} %get-tuple-element.8), channel_id=1, source_target_pairs={{1,0},{2,1},{3,2},{5,4},{6,5},{7,6},{9,8},{10,9},{11,10},{13,12},{... | collective-permute-start | bytes 122888 | tf_op jit(solution)/shard_map/ppermute | solution.py:177
  53.1 1.6 %copy-start.1 = (f32[20,1,512]{2,1,0:T(1,128)}, f32[20,1,512]{2,1,0:T(1,128)S(1)}, u32[]{:S(2)}) copy-start(f32[20,1,512]{2,1,0:T(1,128)S(1)} %collective-permute-done.before_ref) | copy-start | bytes 122884
  54.7 0.6 copy-start.2
  63.6 0.8 %copy-start = (f32[64,5,4,128]{3,2,1,0:T(4,128)}, f32[64,5,4,128]{3,2,1,0:T(4,128)S(1)}, u32[]{:S(2)}) copy-start(f32[64,5,4,128]{3,2,1,0:T(4,128)S(1)} %all-to-all-done.1) | copy-start | bytes 1966084

commit v2 on v1

--- a/solution.py
+++ b/solution.py
@@ -29,9 +29,19 @@
     return np.concatenate([high, high, low], axis=1)
 
 
-def pack_kernel(chunk, parts, x_ref, o_ref):
-    for d in range(parts):
-        o_ref[pl.ds(d * chunk, chunk), :] = x_ref[pl.ds(d, chunk, stride=parts), :]
+def pack_kernel(x_ref, o_ref, held_ref, done_ref):
+    groups, chunk, size, _ = held_ref.shape
+    copies = [
+        pltpu.make_async_copy(x_ref.at[:, pl.ds(g * size, size), :], held_ref.at[g], done_ref.at[g])
+        for g in range(groups)
+    ]
+    for copy in copies:
+        copy.start()
+    for g in range(groups):
+        copies[g].wait()
+        rows = held_ref.at[g].reshape(chunk * size, LANES)
+        for d in range(size):
+            o_ref[pl.ds((g * size + d) * chunk, chunk), :] = rows[pl.ds(d, chunk, stride=size), :]
 
 
 def edge_kernel(x_ref, c_ref, low_ref, high_ref):
@@ -109,10 +119,24 @@
         o_ref[pl.ds(f, total, stride=fields), :] = result[:, f * LANES : (f + 1) * LANES]
 
 
-def combine_kernel(chunk, parts, t_ref, s_ref, o_ref):
-    for q in range(chunk):
-        rows = pl.ds(q * parts, parts)
-        o_ref[rows, :] = t_ref[pl.ds(q, parts, stride=chunk), :] + s_ref[rows, :]
+def combine_kernel(chunk, t_ref, s_ref, o_ref, held_ref, done_ref):
+    groups, size, _ = held_ref.shape
+    parts = groups * size // chunk
+    copies = []
+    for g in range(groups):
+        for q in range(size // parts):
+            tile = g * (size // parts) + q
+            held_ref[g, pl.ds(q * parts, parts), :] = (
+                t_ref[pl.ds(tile, parts, stride=chunk), :] + s_ref[pl.ds(tile * parts, parts), :]
+            )
+        copies.append(
+            pltpu.make_async_copy(
+                held_ref.at[g], o_ref.at[pl.ds(g * size, size), :], done_ref.at[g]
+            )
+        )
+        copies[g].start()
+    for copy in copies:
+        copy.wait()
 
 
 def to_tiles(x):
@@ -134,17 +158,26 @@
     total = local * parts
     chunk = local * fields
     rows = adjoint.size // LANES
-    space = pl.BlockSpec(memory_space=pltpu.VMEM)
-
-    def run(kernel, name, outs, *operands, flops=0):
-        single = isinstance(outs, tuple)
-        shapes = [jax.ShapeDtypeStruct(s, jnp.float32) for s in ([outs] if single else outs)]
-        moved = sum(x.size for x in operands) + sum(s.size for s in shapes)
+    far = pl.BlockSpec(memory_space=pl.ANY)
+    near = pl.BlockSpec(memory_space=pltpu.VMEM)
+    resident = "resident"
+
+    def run(kernel, name, outs, ins, *operands, scratch=(), flops=0):
+        moved = sum(x.size for x in operands) + sum(o.size for o, _ in outs)
+        operands = [
+            pltpu.with_memory_space_constraint(x, pltpu.VMEM) if m is resident else x
+            for x, m in zip(operands, ins)
+        ]
+        shapes = [
+            pltpu.VMEM(o.shape, jnp.float32) if m is resident else o for o, m in outs
+        ]
+        specs = [far if m is far else near for _, m in outs]
         return pl.pallas_call(
             kernel,
-            out_shape=shapes[0] if single else shapes,
-            in_specs=[space] * len(operands),
-            out_specs=space if single else [space] * len(shapes),
+            out_shape=shapes if len(shapes) > 1 else shapes[0],
+            in_specs=[far if m is far else near for m in ins],
+            out_specs=specs if len(specs) > 1 else specs[0],
+            scratch_shapes=list(scratch),
             name=name,
             cost_estimate=pl.CostEstimate(
                 flops=flops, bytes_accessed=4 * moved, transcendentals=0
@@ -155,21 +188,35 @@
         x = x.reshape(parts, fields, local, LANES)
         return lax.all_to_all(x, "inst", 0, 0).reshape(rows, LANES)
 
-    flat = (rows, LANES)
-    packed = run(lambda *r: pack_kernel(chunk, parts, *r), "pack", flat, to_tiles(adjoint))
+    flat = jax.ShapeDtypeStruct((rows, LANES), jnp.float32)
+    groups = parts // SUB
+    packed = run(
+        pack_kernel,
+        "pack",
+        [(flat, resident)],
+        [far],
+        to_tiles(adjoint).reshape(chunk, parts, LANES),
+        scratch=[
+            pltpu.VMEM((groups, chunk, SUB, LANES), jnp.float32),
+            pltpu.SemaphoreType.DMA((groups,)),
+        ],
+    )
     columns = exchange(packed)
     product = run(
         lambda *r: product_kernel(fields, total, *r),
         "time_product",
-        flat,
+        [(flat, resident)],
+        [resident, resident],
         jnp.asarray(derivative_matrix(total)),
         columns,
         flops=6 * total * total * fields * LANES,
     )
     time_part = exchange(product)
 
-    edge = (chunk, 1, radial)
-    first, last = run(edge_kernel, "edges", [edge, edge], adjoint, cell_types)
+    edge = jax.ShapeDtypeStruct((chunk, 1, radial), jnp.float32)
+    first, last = run(
+        edge_kernel, "edges", [(edge, near), (edge, near)], [near, near], adjoint, cell_types
+    )
     count = lax.axis_size("space")
     up = [(i, i + 1) for i in range(count - 1)]
     down = [(i + 1, i) for i in range(count - 1)]
@@ -178,7 +225,8 @@
     rest = run(
         spatial_kernel,
         "spatial",
-        shape,
+        [(jax.ShapeDtypeStruct(shape, jnp.float32), resident)],
+        [near] * 6,
         base_state,
         adjoint,
         gradient,
@@ -187,8 +235,18 @@
         after,
         flops=60 * adjoint.size,
     )
+    pieces = fields
     out = run(
-        lambda *r: combine_kernel(chunk, parts, *r), "combine", flat, time_part, to_tiles(rest)
+        lambda *r: combine_kernel(chunk, *r),
+        "combine",
+        [(flat, far)],
+        [resident, resident],
+        time_part,
+        to_tiles(rest),
+        scratch=[
+            pltpu.VMEM((pieces, rows // pieces, LANES), jnp.float32),
+            pltpu.SemaphoreType.DMA((pieces,)),
+        ],
     )
     return from_tiles(out, shape)
 

time: 67.1 us -> 62.5 us (0.931)
  Pallas kernels: 11.9 us -> 7.5 us
  waiting for transfers between devices: 7.12 us -> 7.97 us
  local copies, waits for them, and re-layouts: 1.46 us -> 0.62 us
    pallas_call x5, Pallas kernels: 11.9 us -> 7.5 us  [run(): pl.pallas_call(kernel, out_shape=shapes if len(shapes) > 1 else shapes[0]...]
    all_to_all x1, waiting for transfers between devices: 5.15 us -> 6 us  [exchange(): return lax.all_to_all(x, 'inst', 0, 0).reshape(rows, LANES)]
    unnamed x6, local copies, waits for them, and re-layouts: 1.46 us -> 0.62 us
  transfers between devices with their start and end apart: 3 -> 3, of which waited for: 3 -> 3; matrix products, arithmetic and copies ran while one was open for 0% -> 0% of each run, Pallas kernels for 7% -> 6%
where the time goes in v2:
time: 62.5 us; the launch traced here: 62.1 us
  blocking collectives  33.1 us (53%)
  starting transfers between devices  12.9 us (21%)
  waiting for transfers between devices  7.97 us (13%)
  Pallas kernels  7.5 us (12%)
    all_to_all x1, blocking collectives, exchange(): return lax.all_to_all(x, 'inst', 0, 0).reshape(rows, LANES)  33.1 us
    pallas_call x5, Pallas kernels, run(): pl.pallas_call(kernel, out_shape=shapes if len(shapes) > 1 else shapes[0]...  7.5 us
    all_to_all x1, waiting for transfers between devices, exchange(): return lax.all_to_all(x, 'inst', 0, 0).reshape(rows, LANES)  6 us
    all_to_all x1, starting transfers between devices, exchange(): return lax.all_to_all(x, 'inst', 0, 0).reshape(rows, LANES)  5.86 us
    ppermute x1, starting transfers between devices, per_device(): after = lax.ppermute(first, 'space', down)  5.15 us
    ppermute x1, starting transfers between devices, per_device(): before = lax.ppermute(last, 'space', up)  1.91 us
    ppermute x1, waiting for transfers between devices, per_device(): after = lax.ppermute(first, 'space', down)  1.63 us
  transfers between devices with their start and end apart: 3, of which 3 were waited for; matrix products, arithmetic and copies ran while one was open for 0% of the time, Pallas kernels for 6%

profile of v2, /device:TPU:16, one launch (start us, length us, event | category | flops | bytes accessed | tf_op | source)
XLA Modules:
  0.0 62.1 jit_solution(16302577436639391605)
XLA Ops:
  0.0 1.3 %pack.1 = f32[1280,128]{1,0:T(8,128)S(1)} custom-call(f32[20,64,128]{2,1,0:T(8,128)} %bitcast.23), custom_call_target="tpu_custom_call" | custom-call | bytes 1310720 | tf_op jit(solution)/shard_map/pack/pallas_call | solution.py:175
  1.3 0.0 copy-start
  1.3 33.1 %all_to_all.10 = f32[64,5,4,128]{3,2,1,0:T(4,128)S(1)} all-to-all(f32[64,5,4,128]{3,2,1,0:T(4,128)S(1)} %bitcast.20), channel_id=1, replica_groups=mesh['inst'=64,'space'=4] {'inst'}, dimensions={0} | all-to-all | bytes 1310720 | tf_op jit(solution)/shard_map/all_to_all | solution.py:189
  34.4 0.0 copy-done
  34.4 1.3 %time_product.1 = f32[1280,128]{1,0:T(8,128)} custom-call(bf16[256,768]{1,0:T(8,128)(2,1)S(1)} %copy-done, f32[1280,128]{1,0:T(8,128)S(1)} %bitcast.19), custom_call_target="tpu_custom_call" | custom-call | flops 251658240 | bytes 2097152 | tf_op jit(solution)/shard_map/time_product/pallas_call | solution.py:175
  35.7 5.9 %all-to-all-start.1 = ((f32[64,5,4,128]{3,2,1,0:T(4,128)}), f32[64,5,4,128]{3,2,1,0:T(4,128)S(1)}, u32[]{:S(2)}, u32[]{:S(2)}) async-start(f32[64,5,4,128]{3,2,1,0:T(4,128)} %bitcast.5), calls=%async_computation.1 | async-start | bytes 1310720 | tf_op jit(solution)/shard_map/all_to_all | solution.py:189
  41.5 1.7 %edges.1 = (f32[20,1,512]{2,1,0:T(1,128)}, f32[20,1,512]{2,1,0:T(1,128)}) custom-call(f32[4,5,16,512]{3,2,1,0:T(8,128)} %adjoint_ref.1, s32[16,512]{1,0:T(8,128)} %cell_ref.1), custom_call_target="tpu_custom_call" | custom-call | bytes 770048 | tf_op jit(solution)/shard_map/edges/pallas_call | solution.py:175
  43.3 1.9 %collective-permute-start = (f32[20,1,512]{2,1,0:T(1,128)}, f32[20,1,512]{2,1,0:T(1,128)S(1)}, u32[]{:S(2)}, u32[]{:S(2)}) collective-permute-start(f32[20,1,512]{2,1,0:T(1,128)} %get-tuple-element.7), channel_id=1, source_target_pairs={{0,1},{1,2},{2,3},{4,5},{5,6},{6,7},{8,9},{9,10},{10,11},{12,13},{... | collective-permute-start | bytes 122888 | tf_op jit(solution)/shard_map/ppermute | solution.py:223
  45.2 5.1 %collective-permute-start.1 = (f32[20,1,512]{2,1,0:T(1,128)}, f32[20,1,512]{2,1,0:T(1,128)S(1)}, u32[]{:S(2)}, u32[]{:S(2)}) collective-permute-start(f32[20,1,512]{2,1,0:T(1,128)} %get-tuple-element.8), channel_id=1, source_target_pairs={{1,0},{2,1},{3,2},{5,4},{6,5},{7,6},{9,8},{10,9},{11,10},{13,12},{... | collective-permute-start | bytes 122888 | tf_op jit(solution)/shard_map/ppermute | solution.py:224
  50.3 0.3 collective-permute-done.before_ref
  50.7 0.0 copy-start.1
  50.7 1.6 %collective-permute-done.1.after_ref = f32[20,1,512]{2,1,0:T(1,128)S(1)} collective-permute-done((f32[20,1,512]{2,1,0:T(1,128)}, f32[20,1,512]{2,1,0:T(1,128)S(1)}, u32[]{:S(2)}, u32[]{:S(2)}) %collective-permute-start.1) | collective-permute-done | bytes 40992 | tf_op jit(solution)/shard_map/ppermute | solution.py:224
  52.3 0.0 copy-done.1
  52.3 0.0 copy-start.2
  52.3 0.6 copy-done.2
  52.9 2.3 %spatial.1 = f32[4,5,16,512]{3,2,1,0:T(8,128)S(1)} custom-call(f32[4,5,16,512]{3,2,1,0:T(8,128)} %state_ref.1, f32[4,5,16,512]{3,2,1,0:T(8,128)} %adjoint_ref.1, f32[4,5,16,512]{3,2,1,0:T(8,128)} %gradient_ref.1, s32[16,512]{1,0:T(8,128)} %cell_ref.1, f32[20,1,512]{2,1,0:T(1,128)} %copy-done.1, f32[20,1,512]{2,1,0:T(1,128)} %copy-done.2), custom_call_target="tpu_custom_call" | custom-call | flops 9830400 | bytes 2736128 | tf_op jit(solution)/shard_map/spatial/pallas_call | solution.py:175
  55.2 6.0 %all-to-all-done.1 = f32[64,5,4,128]{3,2,1,0:T(4,128)S(1)} async-done(((f32[64,5,4,128]{3,2,1,0:T(4,128)}), f32[64,5,4,128]{3,2,1,0:T(4,128)S(1)}, u32[]{:S(2)}, u32[]{:S(2)}) %all-to-all-start.1) | async-done | bytes 655392 | tf_op jit(solution)/shard_map/all_to_all | solution.py:189
  61.2 0.9 %combine.1 = f32[1280,128]{1,0:T(8,128)} custom-call(f32[1280,128]{1,0:T(8,128)S(1)} %bitcast.21, f32[1280,128]{1,0:T(8,128)S(1)} %bitcast.22), custom_call_target="tpu_custom_call" | custom-call | bytes 1966080 | tf_op jit(solution)/shard_map/combine/pallas_call | solution.py:175
Async XLA Ops:
  1.3 33.1 %copy-start = (bf16[256,768]{1,0:T(8,128)(2,1)S(1)}, bf16[256,768]{1,0:T(8,128)(2,1)}, u32[]{:S(2)}) copy-start(bf16[256,768]{1,0:T(8,128)(2,1)} %constant.2.clone.r_0_) | copy-start | bytes 1179652
  35.7 25.6 %all-to-all-start.1 = ((f32[64,5,4,128]{3,2,1,0:T(4,128)}), f32[64,5,4,128]{3,2,1,0:T(4,128)S(1)}, u32[]{:S(2)}, u32[]{:S(2)}) async-start(f32[64,5,4,128]{3,2,1,0:T(4,128)} %bitcast.5), calls=%async_computation.1 | async-start | bytes 1310720 | tf_op jit(solution)/shard_map/all_to_all | solution.py:189
  43.3 7.4 %collective-permute-start = (f32[20,1,512]{2,1,0:T(1,128)}, f32[20,1,512]{2,1,0:T(1,128)S(1)}, u32[]{:S(2)}, u32[]{:S(2)}) collective-permute-start(f32[20,1,512]{2,1,0:T(1,128)} %get-tuple-element.7), channel_id=1, source_target_pairs={{0,1},{1,2},{2,3},{4,5},{5,6},{6,7},{8,9},{9,10},{10,11},{12,13},{... | collective-permute-start | bytes 122888 | tf_op jit(solution)/shard_map/ppermute | solution.py:223
  45.2 7.1 %collective-permute-start.1 = (f32[20,1,512]{2,1,0:T(1,128)}, f32[20,1,512]{2,1,0:T(1,128)S(1)}, u32[]{:S(2)}, u32[]{:S(2)}) collective-permute-start(f32[20,1,512]{2,1,0:T(1,128)} %get-tuple-element.8), channel_id=1, source_target_pairs={{1,0},{2,1},{3,2},{5,4},{6,5},{7,6},{9,8},{10,9},{11,10},{13,12},{... | collective-permute-start | bytes 122888 | tf_op jit(solution)/shard_map/ppermute | solution.py:224
  50.7 1.6 %copy-start.1 = (f32[20,1,512]{2,1,0:T(1,128)}, f32[20,1,512]{2,1,0:T(1,128)S(1)}, u32[]{:S(2)}) copy-start(f32[20,1,512]{2,1,0:T(1,128)S(1)} %collective-permute-done.before_ref) | copy-start | bytes 122884
  52.3 0.6 copy-start.2

commit v3 on v2

--- a/solution.py
+++ b/solution.py
@@ -16,6 +16,7 @@
 
 LANES = 128
 SUB = 8
+FIRST_PART = 43
 
 
 def derivative_matrix(total):
@@ -29,31 +30,41 @@
     return np.concatenate([high, high, low], axis=1)
 
 
-def pack_kernel(x_ref, o_ref, held_ref, done_ref):
+def pack_kernel(across, x_ref, cell_ref, o_ref, edge_ref, held_ref, kinds_ref, done_ref, told_ref):
     groups, chunk, size, _ = held_ref.shape
     copies = [
         pltpu.make_async_copy(x_ref.at[:, pl.ds(g * size, size), :], held_ref.at[g], done_ref.at[g])
         for g in range(groups)
     ]
+    tell = pltpu.make_async_copy(cell_ref, kinds_ref, told_ref)
     for copy in copies:
         copy.start()
+    tell.start()
     for g in range(groups):
         copies[g].wait()
         rows = held_ref.at[g].reshape(chunk * size, LANES)
         for d in range(size):
             o_ref[pl.ds((g * size + d) * chunk, chunk), :] = rows[pl.ds(d, chunk, stride=size), :]
-
-
-def edge_kernel(x_ref, c_ref, low_ref, high_ref):
-    local, fields, axial, _ = x_ref.shape
-    for row, o_ref in ((0, low_ref), (axial - 1, high_ref)):
-        fluid = (c_ref[row : row + 1, :] != 1).astype(jnp.float32)
-        for i in range(local):
-            for f in range(fields):
-                o_ref[i * fields + f] = fluid * x_ref[i, f, row : row + 1, :]
-
-
-def spatial_kernel(state_ref, adjoint_ref, gradient_ref, cell_ref, before_ref, after_ref, o_ref):
+    tell.wait()
+    for side, (first, row) in enumerate(((0, 0), (groups - across, size - 1))):
+        for c in range(across):
+            fluid = (kinds_ref[first + c, row : row + 1, :] != 1).astype(jnp.float32)
+            place = ((first + c) * size + row) * chunk
+            edge_ref[side, c] = fluid * o_ref[pl.ds(place, chunk), :]
+
+
+def spatial_kernel(me_ref, edge_ref, state_ref, adjoint_ref, gradient_ref, cell_ref, o_ref):
+    me = me_ref[0]
+    count, _, across, _, _ = edge_ref.shape
+    below, above = jnp.maximum(me - 1, 0), jnp.minimum(me + 1, count - 1)
+    has_below = (me > 0).astype(jnp.float32)
+    has_above = (me < count - 1).astype(jnp.float32)
+
+    def beyond(member, side, q):
+        return jnp.concatenate(
+            [edge_ref[member, side, c, q : q + 1, :] for c in range(across)], axis=1
+        )
+
     local, fields, axial, radial = state_ref.shape
     cell = cell_ref[...]
     fluid = (cell != 1).astype(jnp.float32)
@@ -66,9 +77,14 @@
         for f in range(fields):
             adjoint = adjoint_ref[i, f]
             weighted = fluid * adjoint
-            before = jnp.where(row == 0, before_ref[i * fields + f], pltpu.roll(weighted, 1, 0))
+            q = i * fields + f
+            before = jnp.where(
+                row == 0, has_below * beyond(below, 1, q), pltpu.roll(weighted, 1, 0)
+            )
             after = jnp.where(
-                row == axial - 1, after_ref[i * fields + f], pltpu.roll(weighted, axial - 1, 0)
+                row == axial - 1,
+                has_above * beyond(above, 0, q),
+                pltpu.roll(weighted, axial - 1, 0),
             )
             inward = jnp.where(lane == 0, 0.0, pltpu.roll(weighted, 1, 1))
             outward = jnp.where(lane == radial - 1, 0.0, pltpu.roll(weighted, radial - 1, 1))
@@ -160,6 +176,7 @@
     rows = adjoint.size // LANES
     far = pl.BlockSpec(memory_space=pl.ANY)
     near = pl.BlockSpec(memory_space=pltpu.VMEM)
+    scalars = pl.BlockSpec(memory_space=pltpu.SMEM)
     resident = "resident"
 
     def run(kernel, name, outs, ins, *operands, scratch=(), flops=0):
@@ -175,7 +192,7 @@
         return pl.pallas_call(
             kernel,
             out_shape=shapes if len(shapes) > 1 else shapes[0],
-            in_specs=[far if m is far else near for m in ins],
+            in_specs=[near if m is resident else m for m in ins],
             out_specs=specs if len(specs) > 1 else specs[0],
             scratch_shapes=list(scratch),
             name=name,
@@ -186,21 +203,30 @@
 
     def exchange(x):
         x = x.reshape(parts, fields, local, LANES)
-        return lax.all_to_all(x, "inst", 0, 0).reshape(rows, LANES)
-
+        return lax.all_to_all(x, "inst", 0, 0, axis_index_groups=[order]).reshape(rows, LANES)
+
+    first_part = FIRST_PART % parts
+    order = [(first_part + p) % parts for p in range(parts)]
     flat = jax.ShapeDtypeStruct((rows, LANES), jnp.float32)
     groups = parts // SUB
-    packed = run(
-        pack_kernel,
+    across = radial // LANES
+    kinds = cell_types.reshape(-1, SUB, across, LANES).transpose(0, 2, 1, 3)
+    edge = jax.ShapeDtypeStruct((2, across, chunk, LANES), jnp.float32)
+    packed, edges = run(
+        lambda *r: pack_kernel(across, *r),
         "pack",
-        [(flat, resident)],
-        [far],
+        [(flat, resident), (edge, resident)],
+        [far, far],
         to_tiles(adjoint).reshape(chunk, parts, LANES),
+        kinds.reshape(groups, SUB, LANES),
         scratch=[
             pltpu.VMEM((groups, chunk, SUB, LANES), jnp.float32),
+            pltpu.VMEM((groups, SUB, LANES), jnp.int32),
             pltpu.SemaphoreType.DMA((groups,)),
+            pltpu.SemaphoreType.DMA,
         ],
     )
+    all_edges = lax.all_gather(edges, "space")
     columns = exchange(packed)
     product = run(
         lambda *r: product_kernel(fields, total, *r),
@@ -213,26 +239,17 @@
     )
     time_part = exchange(product)
 
-    edge = jax.ShapeDtypeStruct((chunk, 1, radial), jnp.float32)
-    first, last = run(
-        edge_kernel, "edges", [(edge, near), (edge, near)], [near, near], adjoint, cell_types
-    )
-    count = lax.axis_size("space")
-    up = [(i, i + 1) for i in range(count - 1)]
-    down = [(i + 1, i) for i in range(count - 1)]
-    before = lax.ppermute(last, "space", up)
-    after = lax.ppermute(first, "space", down)
     rest = run(
         spatial_kernel,
         "spatial",
         [(jax.ShapeDtypeStruct(shape, jnp.float32), resident)],
-        [near] * 6,
+        [scalars] + [near] * 5,
+        lax.axis_index("space").astype(jnp.int32).reshape(1),
+        all_edges,
         base_state,
         adjoint,
         gradient,
         cell_types,
-        before,
-        after,
         flops=60 * adjoint.size,
     )
     pieces = fields

time: 62.5 us -> 58.9 us (0.942)
  blocking collectives: 33.1 us -> 37.9 us
  waiting for transfers between devices: 7.97 us -> 3.27 us
  starting transfers between devices: 12.9 us -> 10.6 us
  Pallas kernels: 7.5 us -> 5.93 us
    all_gather x0 -> x1, blocking collectives: none -> 8.1 us  [per_device(): all_edges = lax.all_gather(edges, 'space')]
    ppermute x2 -> x0, starting transfers between devices: 7.05 us -> none  [the longest x1 5.15 us: per_device(): after = lax.ppermute(first, 'space', down)]
    all_to_all x1, starting transfers between devices: 5.86 us -> 10.6 us  [exchange(): lax.all_to_all(x, 'inst', 0, 0, axis_index_groups=[order])]
    all_to_all x1, blocking collectives: 33.1 us -> 29.8 us  [exchange(): lax.all_to_all(x, 'inst', 0, 0, axis_index_groups=[order])]
    all_to_all x1, waiting for transfers between devices: 6 us -> 3.27 us  [exchange(): lax.all_to_all(x, 'inst', 0, 0, axis_index_groups=[order])]
    ppermute x2 -> x0, waiting for transfers between devices: 1.97 us -> none  [the longest x1 1.63 us: per_device(): after = lax.ppermute(first, 'space', down)]
    pallas_call x5 -> x4, Pallas kernels: 7.5 us -> 5.93 us  [run(): pl.pallas_call(kernel, out_shape=shapes if len(shapes) > 1 else shapes[0]...]
    all_gather x0 -> x1, local copies, waits for them, and re-layouts: none -> 0.79 us  [per_device(): all_edges = lax.all_gather(edges, 'space')]
  transfers between devices with their start and end apart: 3 -> 1, of which waited for: 3 -> 1; matrix products, arithmetic and copies ran while one was open for 0% -> 1% of each run, Pallas kernels for 6% -> 4%
where the time goes in v3:
time: 58.9 us; the launch traced here: 58.6 us
  blocking collectives  37.9 us (64%)
  starting transfers between devices  10.6 us (18%)
  Pallas kernels  5.93 us (10%)
  waiting for transfers between devices  3.27 us (6%)
  local copies, waits for them, and re-layouts  0.82 us (1%)
    all_to_all x1, blocking collectives, exchange(): lax.all_to_all(x, 'inst', 0, 0, axis_index_groups=[order])  29.8 us
    all_to_all x1, starting transfers between devices, exchange(): lax.all_to_all(x, 'inst', 0, 0, axis_index_groups=[order])  10.6 us
    all_gather x1, blocking collectives, per_device(): all_edges = lax.all_gather(edges, 'space')  8.1 us
    pallas_call x4, Pallas kernels, run(): pl.pallas_call(kernel, out_shape=shapes if len(shapes) > 1 else shapes[0]...  5.93 us
    all_to_all x1, waiting for transfers between devices, exchange(): lax.all_to_all(x, 'inst', 0, 0, axis_index_groups=[order])  3.27 us
  transfers between devices with their start and end apart: 1, of which 1 were waited for; matrix products, arithmetic and copies ran while one was open for 1% of the time, Pallas kernels for 4%

profile of v3, /device:TPU:16, one launch (start us, length us, event | category | flops | bytes accessed | tf_op | source)
XLA Modules:
  0.0 58.6 jit_solution(9975439035616105252)
XLA Ops:
  0.0 1.3 %pack.1 = (f32[1280,128]{1,0:T(8,128)S(1)}, f32[2,4,20,128]{3,2,1,0:T(8,128)S(1)}) custom-call(f32[20,64,128]{2,1,0:T(8,128)} %bitcast.30, s32[8,8,128]{2,1,0:T(8,128)} %bitcast.32), custom_call_target="tpu_custom_call" | custom-call | bytes 1425408 | tf_op jit(solution)/shard_map/pack/pallas_call | solution.py:192
  1.3 0.0 copy-start
  1.3 29.8 %all_to_all.10 = f32[64,5,4,128]{3,2,1,0:T(4,128)S(1)} all-to-all(f32[64,5,4,128]{3,2,1,0:T(4,128)S(1)} %bitcast.29), channel_id=1, replica_groups={{172,176,180,184,188,192,196,200,204,208,212,216,220,224,228,232,236,24..., dimensions={0} | all-to-all | bytes 1310720 | tf_op jit(solution)/shard_map/all_to_all | solution.py:206
  31.1 0.0 copy-done
  31.1 1.3 %time_product.1 = f32[1280,128]{1,0:T(8,128)} custom-call(bf16[256,768]{1,0:T(8,128)(2,1)S(1)} %copy-done, f32[1280,128]{1,0:T(8,128)S(1)} %bitcast.27), custom_call_target="tpu_custom_call" | custom-call | flops 251658240 | bytes 2097152 | tf_op jit(solution)/shard_map/time_product/pallas_call | solution.py:192
  32.5 10.6 %all-to-all-start.1 = ((f32[64,5,4,128]{3,2,1,0:T(4,128)}), f32[64,5,4,128]{3,2,1,0:T(4,128)S(1)}, u32[]{:S(2)}, u32[]{:S(2)}) async-start(f32[64,5,4,128]{3,2,1,0:T(4,128)} %bitcast.8), calls=%async_computation.1 | async-start | bytes 1310720 | tf_op jit(solution)/shard_map/all_to_all | solution.py:206
  43.1 8.1 %all-gather = f32[8,4,20,128]{3,1,2,0:T(4,128)S(1)} all-gather(f32[2,4,20,128]{3,1,2,0:T(4,128)S(1)} %copy.6), channel_id=2, replica_groups=mesh['inst'=64,'space'=4] {'space'}, dimensions={0}, use_global_device_ids=true | all-gather | bytes 409600 | tf_op jit(solution)/shard_map/all_gather | solution.py:229
  51.2 0.8 %copy.7 = f32[8,4,20,128]{3,2,1,0:T(8,128)} copy(f32[8,4,20,128]{3,1,2,0:T(4,128)S(1)} %all-gather) | data formatting | bytes 655360 | tf_op jit(solution)/shard_map/all_gather | solution.py:229
  52.0 2.4 %spatial.1 = f32[4,5,16,512]{3,2,1,0:T(8,128)S(1)} custom-call(s32[1]{0:T(128)} %bitcast.10.me_ref, f32[4,2,4,20,128]{4,3,2,1,0:T(8,128)} %bitcast.31, f32[4,5,16,512]{3,2,1,0:T(8,128)} %state_ref.1, f32[4,5,16,512]{3,2,1,0:T(8,128)} %adjoint_ref.1, f32[4,5,16,512]{3,2,1,0:T(8,128)} %gradient_ref.1, s32[16,512]{1,0:T(8,128)} %cell_ref.1), custom_call_target="tpu_custom_call" | custom-call | flops 9830400 | bytes 2981892 | tf_op jit(solution)/shard_map/spatial/pallas_call | solution.py:192
  54.4 3.3 %all-to-all-done.1 = f32[64,5,4,128]{3,2,1,0:T(4,128)S(1)} async-done(((f32[64,5,4,128]{3,2,1,0:T(4,128)}), f32[64,5,4,128]{3,2,1,0:T(4,128)S(1)}, u32[]{:S(2)}, u32[]{:S(2)}) %all-to-all-start.1) | async-done | bytes 655392 | tf_op jit(solution)/shard_map/all_to_all | solution.py:206
  57.7 0.9 %combine.1 = f32[1280,128]{1,0:T(8,128)} custom-call(f32[1280,128]{1,0:T(8,128)S(1)} %bitcast.28, f32[1280,128]{1,0:T(8,128)S(1)} %bitcast.26), custom_call_target="tpu_custom_call" | custom-call | bytes 1966080 | tf_op jit(solution)/shard_map/combine/pallas_call | solution.py:192
  (1 shorter events, 0.0 us)
Async XLA Ops:
  1.3 29.9 %copy-start = (bf16[256,768]{1,0:T(8,128)(2,1)S(1)}, bf16[256,768]{1,0:T(8,128)(2,1)}, u32[]{:S(2)}) copy-start(bf16[256,768]{1,0:T(8,128)(2,1)} %constant.6.clone.r_0_) | copy-start | bytes 1179652
  32.5 25.2 %all-to-all-start.1 = ((f32[64,5,4,128]{3,2,1,0:T(4,128)}), f32[64,5,4,128]{3,2,1,0:T(4,128)S(1)}, u32[]{:S(2)}, u32[]{:S(2)}) async-start(f32[64,5,4,128]{3,2,1,0:T(4,128)} %bitcast.8), calls=%async_computation.1 | async-start | bytes 1310720 | tf_op jit(solution)/shard_map/all_to_all | solution.py:206

commit v4 on v2

v4 whole, which is shorter than its diff:
```python
import jax
import jax.numpy as jnp
import numpy as np
from jax import lax
from jax.experimental import pallas as pl
from jax.experimental.pallas import tpu as pltpu
from jax.sharding import PartitionSpec as P

dissipation = 0.5
ionize_rate = 0.6
collide_rate = 0.4
energy_loss = 0.3
field_push = 0.8
wall_relax = 2.0
time_factor = 4.0

LANES = 128
SUB = 8
FIRST_PART = 43


def derivative_matrix(total):
    gap = np.arange(total)[:, None] - np.arange(total)[None, :]
    off = gap != 0
    angle = np.where(off, np.pi * gap / total, 1.0)
    entry = np.where(off, 0.5 * np.where(gap % 2 == 0, 1.0, -1.0) / np.tan(angle), 0.0)
    entry = -(time_factor / total) * entry
    high = entry.astype(jnp.bfloat16)
    low = (entry - high.astype(np.float64)).astype(jnp.bfloat16)
    return np.concatenate([high, high, low], axis=1)


def interior(
    state_ref, adjoint_ref, gradient_ref, cell_ref, out_ref,
    held_refs, o_ref, held_cell, done_ref, out_done, told,
):
    local, fields, axial, radial = out_ref.shape
    def fetch(i):
        return [
            pltpu.make_async_copy(far_ref.at[i], near_ref.at[i % 2], done_ref.at[i % 2, n])
            for n, (far_ref, near_ref) in enumerate(
                zip((state_ref, adjoint_ref, gradient_ref), held_refs)
            )
        ]

    for copy in fetch(0):
        copy.start()
    kinds = pltpu.make_async_copy(cell_ref, held_cell, told)
    kinds.start()
    kinds.wait()
    cell = held_cell[...]
    fluid = (cell != 1).astype(jnp.float32)
    feed = (cell == 0).astype(jnp.float32) + 3.0 * (cell == 2).astype(jnp.float32)
    relax = wall_relax * (cell == 1).astype(jnp.float32)
    row = lax.broadcasted_iota(jnp.int32, (axial, radial), 0)
    lane = lax.broadcasted_iota(jnp.int32, (axial, radial), 1)
    for i in range(local):
        for copy in fetch(i):
            copy.wait()
        if i + 1 < local:
            for copy in fetch(i + 1):
                copy.start()
        held_state, held_adjoint, held_gradient = (ref.at[i % 2] for ref in held_refs)
        axial_diff, radial_diff, source, spread = [], [], [], []
        for f in range(fields):
            adjoint = held_adjoint[f]
            weighted = fluid * adjoint
            before = jnp.where(row == 0, 0.0, pltpu.roll(weighted, 1, 0))
            after = jnp.where(row == axial - 1, 0.0, pltpu.roll(weighted, axial - 1, 0))
            inward = jnp.where(lane == 0, 0.0, pltpu.roll(weighted, 1, 1))
            outward = jnp.where(lane == radial - 1, 0.0, pltpu.roll(weighted, radial - 1, 1))
            axial_diff.append(0.5 * (after - before))
            radial_diff.append(0.5 * (outward - inward))
            source.append(feed * adjoint)
            spread.append(
                dissipation * ((after + before) + (outward + inward))
                - (4.0 * dissipation) * weighted
                - relax * adjoint
                - held_gradient[f]
            )
        ion = jnp.exp(held_state[0])
        u = held_state[1]
        v = held_state[2]
        neutral = jnp.exp(held_state[3])
        temper = held_state[4]
        p, q, m = axial_diff, radial_diff, source
        ionize = ionize_rate * neutral * (m[0] - m[3])
        if i > 0:
            out.wait()
        o_ref[0] = spread[0] + ion * (u * p[0] + v * q[0])
        o_ref[1] = (
            spread[1]
            + (ion * p[0] + u * p[1] + v * (p[2] + q[1]) + temper * p[4])
            + (field_push * m[4] - collide_rate * m[1])
        )
        o_ref[2] = (
            spread[2]
            + (ion * q[0] + u * (p[2] + q[1]) + v * q[2] + 0.5 * neutral * q[3] + temper * q[4])
            - collide_rate * m[2]
        )
        o_ref[3] = spread[3] + neutral * (p[3] + 0.5 * v * q[3]) + ionize * temper
        o_ref[4] = (
            spread[4]
            + (p[1] + q[2] + u * p[4] + v * q[4])
            + (ionize + field_push * m[1] - (2.0 * energy_loss) * temper * m[4])
        )
        out = pltpu.make_async_copy(o_ref, out_ref.at[i], out_done)
        out.start()
    out.wait()


def pack_kernel(
    across, me_ref, x_ref, kind_ref, state_ref, adjoint_ref, gradient_ref, cell_ref,
    o_ref, edge_ref, rest_ref,
    held_ref, kinds_ref, done_ref, told_ref, *work,
):
    groups, chunk, size, _ = held_ref.shape

    copies = [
        pltpu.make_async_copy(x_ref.at[:, pl.ds(g * size, size), :], held_ref.at[g], done_ref.at[g])
        for g in range(groups)
    ]
    tell = pltpu.make_async_copy(kind_ref, kinds_ref, told_ref)
    for copy in copies:
        copy.start()
    tell.start()
    @pl.when(me_ref[0] % 2 == 0)
    def _():
        interior(
            state_ref, adjoint_ref, gradient_ref, cell_ref, rest_ref, work[:3], *work[3:]
        )

    for g in range(groups):
        copies[g].wait()
        rows = held_ref.at[g].reshape(chunk * size, LANES)
        for d in range(size):
            o_ref[pl.ds((g * size + d) * chunk, chunk), :] = rows[pl.ds(d, chunk, stride=size), :]
    tell.wait()
    for side, (first, row) in enumerate(((0, 0), (groups - across, size - 1))):
        for c in range(across):
            fluid = (kinds_ref[first + c, row : row + 1, :] != 1).astype(jnp.float32)
            place = ((first + c) * size + row) * chunk
            edge_ref[pl.ds((side * across + c) * chunk, chunk), :] = (
                fluid * o_ref[pl.ds(place, chunk), :]
            )


def interior_kernel(
    me_ref, early_ref, edge_ref, state_ref, adjoint_ref, gradient_ref, cell_ref,
    rest_ref, edges_ref, *work,
):
    del early_ref, edge_ref, edges_ref

    @pl.when(me_ref[0] % 2 == 1)
    def _():
        interior(
            state_ref, adjoint_ref, gradient_ref, cell_ref, rest_ref, work[:3], *work[3:]
        )


def border_kernel(before_ref, after_ref, state_ref, o_ref):
    local, fields, axial, radial = state_ref.shape
    across, chunk = radial // LANES, local * fields
    sides = ((0, -0.5, before_ref), (axial - 1, 0.5, after_ref))
    for mine, (row, sign, edge_ref) in enumerate(sides):
        for c in range(across):
            lanes = pl.ds(c * LANES, LANES)
            edges = [
                edge_ref[pl.ds(c * chunk + f, local, stride=fields), :] for f in range(fields)
            ]
            ion, u, v, neutral, temper = [state_ref[:, f, row, lanes] for f in range(fields)]
            ion, neutral = jnp.exp(ion), jnp.exp(neutral)
            p = [sign * e for e in edges]
            added = (
                ion * u * p[0],
                ion * p[0] + u * p[1] + v * p[2] + temper * p[4],
                u * p[2],
                neutral * p[3],
                p[1] + u * p[4],
            )
            for f in range(fields):
                total = dissipation * edges[f] + added[f]
                for i in range(local):
                    o_ref[mine, i * fields + f, c : c + 1, :] = total[i : i + 1, :]


def product_kernel(fields, total, d_ref, x_ref, o_ref):
    columns = jnp.concatenate(
        [x_ref[pl.ds(f, total, stride=fields), :] for f in range(fields)], axis=1
    )
    high = columns.astype(jnp.bfloat16)
    low = (columns - high.astype(jnp.float32)).astype(jnp.bfloat16)
    stacked = jnp.concatenate([high, low, high], axis=0)
    result = jnp.dot(d_ref[...], stacked, preferred_element_type=jnp.float32)
    for f in range(fields):
        o_ref[pl.ds(f, total, stride=fields), :] = result[:, f * LANES : (f + 1) * LANES]


def combine_kernel(chunk, t_ref, s_ref, b_ref, o_ref, held_ref, done_ref):
    groups, size, _ = held_ref.shape
    parts = groups * size // chunk
    copies = []
    for g in range(groups):
        for q in range(size // parts):
            tile = g * (size // parts) + q
            held_ref[g, pl.ds(q * parts, parts), :] = (
                t_ref[pl.ds(tile, parts, stride=chunk), :] + s_ref[pl.ds(tile * parts, parts), :]
            )
            across = b_ref.shape[2]
            for side, at in ((0, 0), (1, parts - across * SUB + SUB - 1)):
                held_ref[g, pl.ds(q * parts + at, across, stride=SUB), :] += b_ref[side, tile]
        copies.append(
            pltpu.make_async_copy(
                held_ref.at[g], o_ref.at[pl.ds(g * size, size), :], done_ref.at[g]
            )
        )
        copies[g].start()
    for copy in copies:
        copy.wait()


def to_tiles(x):
    local, fields, axial, radial = x.shape
    x = x.reshape(local, fields, axial // SUB, SUB, radial // LANES, LANES)
    return x.transpose(0, 1, 2, 4, 3, 5).reshape(-1, LANES)


def from_tiles(x, shape):
    local, fields, axial, radial = shape
    x = x.reshape(local, fields, axial // SUB, radial // LANES, SUB, LANES)
    return x.transpose(0, 1, 2, 4, 3, 5).reshape(shape)


def per_device(base_state, adjoint, gradient, cell_types):
    shape = adjoint.shape
    local, fields, _, radial = shape
    parts = lax.axis_size("inst")
    total = local * parts
    chunk = local * fields
    rows = adjoint.size // LANES
    far = pl.BlockSpec(memory_space=pl.ANY)
    near = pl.BlockSpec(memory_space=pltpu.VMEM)
    scalars = pl.BlockSpec(memory_space=pltpu.SMEM)
    resident = "resident"

    def run(kernel, name, outs, ins, *operands, scratch=(), flops=0, aliases=None):
        moved = sum(x.size for x in operands) + sum(o.size for o, _ in outs)
        operands = [
            pltpu.with_memory_space_constraint(x, pltpu.VMEM) if m is resident else x
            for x, m in zip(operands, ins)
        ]
        shapes = [
            pltpu.VMEM(o.shape, jnp.float32) if m is resident else o for o, m in outs
        ]
        specs = [far if m is far else near for _, m in outs]
        return pl.pallas_call(
            kernel,
            out_shape=shapes if len(shapes) > 1 else shapes[0],
            in_specs=[near if m is resident else m for m in ins],
            out_specs=specs if len(specs) > 1 else specs[0],
            scratch_shapes=list(scratch),
            input_output_aliases=aliases or {},
            name=name,
            cost_estimate=pl.CostEstimate(
                flops=flops, bytes_accessed=4 * moved, transcendentals=0
            ),
        )(*operands)

    def exchange(x):
        x = x.reshape(parts, fields, local, LANES)
        return lax.all_to_all(x, "inst", 0, 0, axis_index_groups=[order]).reshape(rows, LANES)

    first_part = FIRST_PART % parts
    order = [(first_part + p) % parts for p in range(parts)]
    flat = jax.ShapeDtypeStruct((rows, LANES), jnp.float32)
    groups = parts // SUB
    across = radial // LANES
    kinds = cell_types.reshape(-1, SUB, across, LANES).transpose(0, 2, 1, 3)
    edge = jax.ShapeDtypeStruct((2 * across * chunk, LANES), jnp.float32)
    me = lax.axis_index("space").astype(jnp.int32).reshape(1)
    whole = jax.ShapeDtypeStruct(shape, jnp.float32)
    work = [
        *[pltpu.VMEM((2, *shape[1:]), jnp.float32)] * 3,
        pltpu.VMEM(shape[1:], jnp.float32),
        pltpu.VMEM(shape[2:], jnp.int32),
        pltpu.SemaphoreType.DMA((2, 3)),
        pltpu.SemaphoreType.DMA,
        pltpu.SemaphoreType.DMA,
    ]
    packed, edges, early = run(
        lambda *r: pack_kernel(across, *r),
        "pack",
        [(flat, resident), (edge, resident), (whole, far)],
        [scalars] + [far] * 6,
        me,
        to_tiles(adjoint).reshape(chunk, parts, LANES),
        kinds.reshape(groups, SUB, LANES),
        base_state,
        adjoint,
        gradient,
        cell_types,
        scratch=[
            pltpu.VMEM((groups, chunk, SUB, LANES), jnp.float32),
            pltpu.VMEM((groups, SUB, LANES), jnp.int32),
            pltpu.SemaphoreType.DMA((groups,)),
            pltpu.SemaphoreType.DMA,
            *work,
        ],
    )
    columns = exchange(packed)
    product = run(
        lambda *r: product_kernel(fields, total, *r),
        "time_product",
        [(flat, resident)],
        [resident, resident],
        jnp.asarray(derivative_matrix(total)),
        columns,
        flops=6 * total * total * fields * LANES,
    )
    time_part = exchange(product)

    inner, edges = run(
        interior_kernel,
        "interior",
        [(whole, far), (edge, resident)],
        [scalars, far, resident, far, far, far, far],
        me,
        early,
        edges,
        base_state,
        adjoint,
        gradient,
        cell_types,
        scratch=work,
        flops=60 * adjoint.size,
        aliases={1: 0, 2: 1},
    )
    count = lax.axis_size("space")
    half = across * chunk
    up = [(i, i + 1) for i in range(count - 1)]
    down = [(i + 1, i) for i in range(count - 1)]
    borders = run(
        border_kernel,
        "border",
        [(jax.ShapeDtypeStruct((2, chunk, across, LANES), jnp.float32), resident)],
        [resident] * 3,
        lax.ppermute(edges[half:], "space", up),
        lax.ppermute(edges[:half], "space", down),
        base_state,
        flops=4 * adjoint.size,
    )
    pieces = fields
    out = run(
        lambda *r: combine_kernel(chunk, *r),
        "combine",
        [(flat, far)],
        [resident, resident, resident],
        time_part,
        to_tiles(inner),
        borders,
        scratch=[
            pltpu.VMEM((pieces, rows // pieces, LANES), jnp.float32),
            pltpu.SemaphoreType.DMA((pieces,)),
        ],
    )
    return from_tiles(out, shape)


def solution(mesh):
    return jax.shard_map(
        per_device,
        mesh=mesh,
        in_specs=(
            P("inst", None, "space", None),
            P("inst", None, "space", None),
            P("inst", None, "space", None),
            P("space", None),
        ),
        out_specs=P("inst", None, "space", None),
        check_vma=False,
    )
```

time: 62.5 us -> 55.4 us (0.89)
  blocking collectives: 33.1 us -> 25.3 us
  starting transfers between devices: 12.9 us -> 14.9 us
  waiting for transfers between devices: 7.97 us -> 6.57 us
  Pallas kernels: 7.5 us -> 8.16 us
    all_to_all x1, blocking collectives: 33.1 us -> 25.3 us  [exchange(): lax.all_to_all(x, 'inst', 0, 0, axis_index_groups=[order])]
    all_to_all x1, starting transfers between devices: 5.86 us -> 10.4 us  [exchange(): lax.all_to_all(x, 'inst', 0, 0, axis_index_groups=[order])]
    all_to_all x1, waiting for transfers between devices: 6 us -> 1.99 us  [exchange(): lax.all_to_all(x, 'inst', 0, 0, axis_index_groups=[order])]
    ppermute x2, waiting for transfers between devices: 1.97 us -> 4.58 us  [the longest x1 4.57 us: per_device(): lax.ppermute(edges[half:], 'space', up)]
    ppermute x2, starting transfers between devices: 7.05 us -> 4.46 us  [the longest x1 2.34 us: per_device(): lax.ppermute(edges[half:], 'space', up)]
    pallas_call x5, Pallas kernels: 7.5 us -> 8.16 us  [run(): pl.pallas_call(kernel, out_shape=shapes if len(shapes) > 1 else shapes[0]...]
  transfers between devices with their start and end apart: 3 -> 3, of which waited for: 3 -> 2; matrix products, arithmetic and copies ran while one was open for 0% -> 0% of each run, Pallas kernels for 6% -> 0%
where the time goes in v4:
time: 55.4 us; the launch traced here: 55.1 us
  blocking collectives  25.3 us (46%)
  starting transfers between devices  14.9 us (27%)
  Pallas kernels  8.16 us (15%)
  waiting for transfers between devices  6.57 us (12%)
    all_to_all x1, blocking collectives, exchange(): lax.all_to_all(x, 'inst', 0, 0, axis_index_groups=[order])  25.3 us
    all_to_all x1, starting transfers between devices, exchange(): lax.all_to_all(x, 'inst', 0, 0, axis_index_groups=[order])  10.4 us
    pallas_call x5, Pallas kernels, run(): pl.pallas_call(kernel, out_shape=shapes if len(shapes) > 1 else shapes[0]...  8.16 us
    ppermute x1, waiting for transfers between devices, per_device(): lax.ppermute(edges[half:], 'space', up)  4.57 us
    ppermute x1, starting transfers between devices, per_device(): lax.ppermute(edges[half:], 'space', up)  2.34 us
    ppermute x1, starting transfers between devices, per_device(): lax.ppermute(edges[:half], 'space', down)  2.11 us
    all_to_all x1, waiting for transfers between devices, exchange(): lax.all_to_all(x, 'inst', 0, 0, axis_index_groups=[order])  1.99 us
  transfers between devices with their start and end apart: 3, of which 2 were waited for; matrix products, arithmetic and copies ran while one was open for 0% of the time, Pallas kernels for 0%

profile of v4, /device:TPU:16, one launch (start us, length us, event | category | flops | bytes accessed | tf_op | source)
XLA Modules:
  0.0 55.1 jit_solution(2625889709284452728)
XLA Ops:
  0.0 5.8 %pack.1 = (f32[1280,128]{1,0:T(8,128)S(1)}, f32[160,128]{1,0:T(8,128)S(1)}, f32[4,5,16,512]{3,2,1,0:T(8,128)}) custom-call(s32[1]{0:T(128)} %bitcast.r_0_.me_ref, f32[20,64,128]{2,1,0:T(8,128)} %bitcast.29, s32[8,8,128]{2,1,0:T(8,128)} %bitcast.30, f32[4,5,16,512]{3,2,1,0:T(8,128)} %state_ref.3, f32[4,5,16,512]{3,2,1,0:T(8,128)} %adjoint_ref.1, ...), custom_call_target="tpu_custom_call" | custom-call | bytes 4079620 | tf_op jit(solution)/shard_map/pack/pallas_call | solution.py:256
  5.8 0.0 copy-start.2
  5.8 25.3 %all_to_all.10 = f32[64,5,4,128]{3,2,1,0:T(4,128)S(1)} all-to-all(f32[64,5,4,128]{3,2,1,0:T(4,128)S(1)} %bitcast.28), channel_id=1, replica_groups={{172,176,180,184,188,192,196,200,204,208,212,216,220,224,228,232,236,24..., dimensions={0} | all-to-all | bytes 1310720 | tf_op jit(solution)/shard_map/all_to_all | solution.py:271
  31.1 0.0 copy-done.2
  31.1 1.3 %time_product.1 = f32[1280,128]{1,0:T(8,128)} custom-call(bf16[256,768]{1,0:T(8,128)(2,1)S(1)} %copy-done.2, f32[1280,128]{1,0:T(8,128)S(1)} %bitcast.26), custom_call_target="tpu_custom_call" | custom-call | flops 251658240 | bytes 2097152 | tf_op jit(solution)/shard_map/time_product/pallas_call | solution.py:256
  32.4 10.4 %all-to-all-start.1 = ((f32[64,5,4,128]{3,2,1,0:T(4,128)}), f32[64,5,4,128]{3,2,1,0:T(4,128)S(1)}, u32[]{:S(2)}, u32[]{:S(2)}) async-start(f32[64,5,4,128]{3,2,1,0:T(4,128)} %bitcast.9), calls=%async_computation.1 | async-start | bytes 1310720 | tf_op jit(solution)/shard_map/all_to_all | solution.py:271
  42.9 0.0 copy-start
  42.9 0.1 interior.1
  43.0 0.0 copy-start.1
  43.0 2.1 %collective-permute-start.1 = (f32[80,128]{1,0:T(8,128)S(1)}, f32[80,128]{1,0:T(8,128)S(1)}, u32[]{:S(2)}, u32[]{:S(2)}) collective-permute-start(f32[80,128]{1,0:T(8,128)S(1)} %get-tuple-element.15), channel_id=1, source_target_pairs={{1,0},{2,1},{3,2},{5,4},{6,5},{7,6},{9,8},{10,9},{11,10},{13,12},{... | collective-permute-start | bytes 122888 | tf_op jit(solution)/shard_map/ppermute | solution.py:348
  45.1 2.3 %collective-permute-start = (f32[80,128]{1,0:T(8,128)S(1)}, f32[80,128]{1,0:T(8,128)S(1)}, u32[]{:S(2)}, u32[]{:S(2)}) collective-permute-start(f32[80,128]{1,0:T(8,128)S(1)} %get-tuple-element.16), channel_id=1, source_target_pairs={{0,1},{1,2},{2,3},{4,5},{5,6},{6,7},{8,9},{9,10},{10,11},{12,13},{... | collective-permute-start | bytes 122888 | tf_op jit(solution)/shard_map/ppermute | solution.py:347
  47.5 0.0 collective-permute-done.1.after_ref
  47.5 4.6 %collective-permute-done.before_ref = f32[80,128]{1,0:T(8,128)S(1)} collective-permute-done((f32[80,128]{1,0:T(8,128)S(1)}, f32[80,128]{1,0:T(8,128)S(1)}, u32[]{:S(2)}, u32[]{:S(2)}) %collective-permute-start) | collective-permute-done | bytes 40992 | tf_op jit(solution)/shard_map/ppermute | solution.py:347
  52.1 0.0 copy-done
  52.1 0.1 border.1.r_2_
  52.2 2.0 %all-to-all-done.1 = f32[64,5,4,128]{3,2,1,0:T(4,128)S(1)} async-done(((f32[64,5,4,128]{3,2,1,0:T(4,128)}), f32[64,5,4,128]{3,2,1,0:T(4,128)S(1)}, u32[]{:S(2)}, u32[]{:S(2)}) %all-to-all-start.1) | async-done | bytes 655392 | tf_op jit(solution)/shard_map/all_to_all | solution.py:271
  54.2 0.0 copy-done.1
  54.2 0.9 %combine.1 = f32[1280,128]{1,0:T(8,128)} custom-call(f32[1280,128]{1,0:T(8,128)S(1)} %bitcast.25, f32[1280,128]{1,0:T(8,128)S(1)} %bitcast.27, f32[2,20,4,128]{3,2,1,0:T(4,128)S(1)} %border.1.r_2_), custom_call_target="tpu_custom_call" | custom-call | bytes 2048000 | tf_op jit(solution)/shard_map/combine/pallas_call | solution.py:256
  (1 shorter events, 0.0 us)
Async XLA Ops:
  5.8 25.3 %copy-start.2 = (bf16[256,768]{1,0:T(8,128)(2,1)S(1)}, bf16[256,768]{1,0:T(8,128)(2,1)}, u32[]{:S(2)}) copy-start(bf16[256,768]{1,0:T(8,128)(2,1)} %constant.6.clone.r_0_) | copy-start | bytes 1179652
  32.4 21.7 %all-to-all-start.1 = ((f32[64,5,4,128]{3,2,1,0:T(4,128)}), f32[64,5,4,128]{3,2,1,0:T(4,128)S(1)}, u32[]{:S(2)}, u32[]{:S(2)}) async-start(f32[64,5,4,128]{3,2,1,0:T(4,128)} %bitcast.9), calls=%async_computation.1 | async-start | bytes 1310720 | tf_op jit(solution)/shard_map/all_to_all | solution.py:271
  42.9 9.2 %copy-start = (f32[4,5,16,512]{3,2,1,0:T(8,128)S(1)}, f32[4,5,16,512]{3,2,1,0:T(8,128)}, u32[]{:S(2)}) copy-start(f32[4,5,16,512]{3,2,1,0:T(8,128)} %state_ref.3) | copy-start | bytes 1966084
  43.0 11.2 %copy-start.1 = (f32[4,5,16,512]{3,2,1,0:T(8,128)S(1)}, f32[4,5,16,512]{3,2,1,0:T(8,128)}, u32[]{:S(2)}) copy-start(f32[4,5,16,512]{3,2,1,0:T(8,128)} %get-tuple-element.13) | copy-start | bytes 1966084
  43.0 4.5 %collective-permute-start.1 = (f32[80,128]{1,0:T(8,128)S(1)}, f32[80,128]{1,0:T(8,128)S(1)}, u32[]{:S(2)}, u32[]{:S(2)}) collective-permute-start(f32[80,128]{1,0:T(8,128)S(1)} %get-tuple-element.15), channel_id=1, source_target_pairs={{1,0},{2,1},{3,2},{5,4},{6,5},{7,6},{9,8},{10,9},{11,10},{13,12},{... | collective-permute-start | bytes 122888 | tf_op jit(solution)/shard_map/ppermute | solution.py:348
  45.1 6.9 %collective-permute-start = (f32[80,128]{1,0:T(8,128)S(1)}, f32[80,128]{1,0:T(8,128)S(1)}, u32[]{:S(2)}, u32[]{:S(2)}) collective-permute-start(f32[80,128]{1,0:T(8,128)S(1)} %get-tuple-element.16), channel_id=1, source_target_pairs={{0,1},{1,2},{2,3},{4,5},{5,6},{6,7},{8,9},{9,10},{10,11},{12,13},{... | collective-permute-start | bytes 122888 | tf_op jit(solution)/shard_map/ppermute | solution.py:347

commit v5 on v4

--- a/solution.py
+++ b/solution.py
@@ -16,7 +16,7 @@
 
 LANES = 128
 SUB = 8
-FIRST_PART = 43
+FIRST_PART = 47
 
 
 def derivative_matrix(total):

time: 55.4 us -> 54.2 us (0.978)
  waiting for transfers between devices: 6.57 us -> 5.02 us
  blocking collectives: 25.3 us -> 24.6 us
  starting transfers between devices: 14.9 us -> 15.5 us
    all_to_all x1, waiting for transfers between devices: 1.99 us -> 0.62 us  [exchange(): lax.all_to_all(x, 'inst', 0, 0, axis_index_groups=[order])]
    all_to_all x1, blocking collectives: 25.3 us -> 24.6 us  [exchange(): lax.all_to_all(x, 'inst', 0, 0, axis_index_groups=[order])]
    all_to_all x1, starting transfers between devices: 10.4 us -> 11 us  [exchange(): lax.all_to_all(x, 'inst', 0, 0, axis_index_groups=[order])]
where the time goes in v5:
time: 54.2 us; the launch traced here: 53.4 us
  blocking collectives  24.6 us (45%)
  starting transfers between devices  15.5 us (29%)
  Pallas kernels  8.16 us (15%)
  waiting for transfers between devices  5.02 us (9%)
    all_to_all x1, blocking collectives, exchange(): lax.all_to_all(x, 'inst', 0, 0, axis_index_groups=[order])  24.6 us
    all_to_all x1, starting transfers between devices, exchange(): lax.all_to_all(x, 'inst', 0, 0, axis_index_groups=[order])  11 us
    pallas_call x5, Pallas kernels, run(): pl.pallas_call(kernel, out_shape=shapes if len(shapes) > 1 else shapes[0]...  8.16 us
    ppermute x1, waiting for transfers between devices, per_device(): lax.ppermute(edges[half:], 'space', up)  4.4 us
    ppermute x1, starting transfers between devices, per_device(): lax.ppermute(edges[half:], 'space', up)  2.4 us
    ppermute x1, starting transfers between devices, per_device(): lax.ppermute(edges[:half], 'space', down)  2.05 us
  transfers between devices with their start and end apart: 3, of which 2 were waited for; matrix products, arithmetic and copies ran while one was open for 0% of the time, Pallas kernels for 0%

profile of v5, /device:TPU:16, one launch (start us, length us, event | category | flops | bytes accessed | tf_op | source)
XLA Modules:
  0.0 53.4 jit_solution(803616657884951356)
XLA Ops:
  0.0 5.8 %pack.1 = (f32[1280,128]{1,0:T(8,128)S(1)}, f32[160,128]{1,0:T(8,128)S(1)}, f32[4,5,16,512]{3,2,1,0:T(8,128)}) custom-call(s32[1]{0:T(128)} %bitcast.r_0_.me_ref, f32[20,64,128]{2,1,0:T(8,128)} %bitcast.29, s32[8,8,128]{2,1,0:T(8,128)} %bitcast.30, f32[4,5,16,512]{3,2,1,0:T(8,128)} %state_ref.3, f32[4,5,16,512]{3,2,1,0:T(8,128)} %adjoint_ref.1, ...), custom_call_target="tpu_custom_call" | custom-call | bytes 4079620 | tf_op jit(solution)/shard_map/pack/pallas_call | solution.py:256
  5.8 0.0 copy-start.2
  5.8 24.6 %all_to_all.10 = f32[64,5,4,128]{3,2,1,0:T(4,128)S(1)} all-to-all(f32[64,5,4,128]{3,2,1,0:T(4,128)S(1)} %bitcast.28), channel_id=1, replica_groups={{188,192,196,200,204,208,212,216,220,224,228,232,236,240,244,248,252,0,..., dimensions={0} | all-to-all | bytes 1310720 | tf_op jit(solution)/shard_map/all_to_all | solution.py:271
  30.3 0.0 copy-done.2
  30.3 1.3 %time_product.1 = f32[1280,128]{1,0:T(8,128)} custom-call(bf16[256,768]{1,0:T(8,128)(2,1)S(1)} %copy-done.2, f32[1280,128]{1,0:T(8,128)S(1)} %bitcast.26), custom_call_target="tpu_custom_call" | custom-call | flops 251658240 | bytes 2097152 | tf_op jit(solution)/shard_map/time_product/pallas_call | solution.py:256
  31.7 11.0 %all-to-all-start.1 = ((f32[64,5,4,128]{3,2,1,0:T(4,128)}), f32[64,5,4,128]{3,2,1,0:T(4,128)S(1)}, u32[]{:S(2)}, u32[]{:S(2)}) async-start(f32[64,5,4,128]{3,2,1,0:T(4,128)} %bitcast.9), calls=%async_computation.1 | async-start | bytes 1310720 | tf_op jit(solution)/shard_map/all_to_all | solution.py:271
  42.7 0.0 copy-start
  42.7 0.1 interior.1
  42.8 0.0 copy-start.1
  42.8 2.1 %collective-permute-start.1 = (f32[80,128]{1,0:T(8,128)S(1)}, f32[80,128]{1,0:T(8,128)S(1)}, u32[]{:S(2)}, u32[]{:S(2)}) collective-permute-start(f32[80,128]{1,0:T(8,128)S(1)} %get-tuple-element.15), channel_id=1, source_target_pairs={{1,0},{2,1},{3,2},{5,4},{6,5},{7,6},{9,8},{10,9},{11,10},{13,12},{... | collective-permute-start | bytes 122888 | tf_op jit(solution)/shard_map/ppermute | solution.py:348
  44.9 2.4 %collective-permute-start = (f32[80,128]{1,0:T(8,128)S(1)}, f32[80,128]{1,0:T(8,128)S(1)}, u32[]{:S(2)}, u32[]{:S(2)}) collective-permute-start(f32[80,128]{1,0:T(8,128)S(1)} %get-tuple-element.16), channel_id=1, source_target_pairs={{0,1},{1,2},{2,3},{4,5},{5,6},{6,7},{8,9},{9,10},{10,11},{12,13},{... | collective-permute-start | bytes 122888 | tf_op jit(solution)/shard_map/ppermute | solution.py:347
  47.3 0.0 collective-permute-done.1.after_ref
  47.3 4.4 %collective-permute-done.before_ref = f32[80,128]{1,0:T(8,128)S(1)} collective-permute-done((f32[80,128]{1,0:T(8,128)S(1)}, f32[80,128]{1,0:T(8,128)S(1)}, u32[]{:S(2)}, u32[]{:S(2)}) %collective-permute-start) | collective-permute-done | bytes 40992 | tf_op jit(solution)/shard_map/ppermute | solution.py:347
  51.7 0.0 copy-done
  51.7 0.1 border.1.r_2_
  51.8 0.6 %all-to-all-done.1 = f32[64,5,4,128]{3,2,1,0:T(4,128)S(1)} async-done(((f32[64,5,4,128]{3,2,1,0:T(4,128)}), f32[64,5,4,128]{3,2,1,0:T(4,128)S(1)}, u32[]{:S(2)}, u32[]{:S(2)}) %all-to-all-start.1) | async-done | bytes 655392 | tf_op jit(solution)/shard_map/all_to_all | solution.py:271
  52.4 0.0 copy-done.1
  52.4 0.9 %combine.1 = f32[1280,128]{1,0:T(8,128)} custom-call(f32[1280,128]{1,0:T(8,128)S(1)} %bitcast.25, f32[1280,128]{1,0:T(8,128)S(1)} %bitcast.27, f32[2,20,4,128]{3,2,1,0:T(4,128)S(1)} %border.1.r_2_), custom_call_target="tpu_custom_call" | custom-call | bytes 2048000 | tf_op jit(solution)/shard_map/combine/pallas_call | solution.py:256
  (1 shorter events, 0.0 us)
Async XLA Ops:
  5.8 24.6 %copy-start.2 = (bf16[256,768]{1,0:T(8,128)(2,1)S(1)}, bf16[256,768]{1,0:T(8,128)(2,1)}, u32[]{:S(2)}) copy-start(bf16[256,768]{1,0:T(8,128)(2,1)} %constant.6.clone.r_0_) | copy-start | bytes 1179652
  31.7 20.8 %all-to-all-start.1 = ((f32[64,5,4,128]{3,2,1,0:T(4,128)}), f32[64,5,4,128]{3,2,1,0:T(4,128)S(1)}, u32[]{:S(2)}, u32[]{:S(2)}) async-start(f32[64,5,4,128]{3,2,1,0:T(4,128)} %bitcast.9), calls=%async_computation.1 | async-start | bytes 1310720 | tf_op jit(solution)/shard_map/all_to_all | solution.py:271
  42.7 9.0 %copy-start = (f32[4,5,16,512]{3,2,1,0:T(8,128)S(1)}, f32[4,5,16,512]{3,2,1,0:T(8,128)}, u32[]{:S(2)}) copy-start(f32[4,5,16,512]{3,2,1,0:T(8,128)} %state_ref.3) | copy-start | bytes 1966084
  42.8 9.6 %copy-start.1 = (f32[4,5,16,512]{3,2,1,0:T(8,128)S(1)}, f32[4,5,16,512]{3,2,1,0:T(8,128)}, u32[]{:S(2)}) copy-start(f32[4,5,16,512]{3,2,1,0:T(8,128)} %get-tuple-element.13) | copy-start | bytes 1966084
  42.8 4.5 %collective-permute-start.1 = (f32[80,128]{1,0:T(8,128)S(1)}, f32[80,128]{1,0:T(8,128)S(1)}, u32[]{:S(2)}, u32[]{:S(2)}) collective-permute-start(f32[80,128]{1,0:T(8,128)S(1)} %get-tuple-element.15), channel_id=1, source_target_pairs={{1,0},{2,1},{3,2},{5,4},{6,5},{7,6},{9,8},{10,9},{11,10},{13,12},{... | collective-permute-start | bytes 122888 | tf_op jit(solution)/shard_map/ppermute | solution.py:348
  44.9 6.8 %collective-permute-start = (f32[80,128]{1,0:T(8,128)S(1)}, f32[80,128]{1,0:T(8,128)S(1)}, u32[]{:S(2)}, u32[]{:S(2)}) collective-permute-start(f32[80,128]{1,0:T(8,128)S(1)} %get-tuple-element.16), channel_id=1, source_target_pairs={{0,1},{1,2},{2,3},{4,5},{5,6},{6,7},{8,9},{9,10},{10,11},{12,13},{... | collective-permute-start | bytes 122888 | tf_op jit(solution)/shard_map/ppermute | solution.py:347

commit v6 on v5

--- a/solution.py
+++ b/solution.py
@@ -57,9 +57,6 @@
     for i in range(local):
         for copy in fetch(i):
             copy.wait()
-        if i + 1 < local:
-            for copy in fetch(i + 1):
-                copy.start()
         held_state, held_adjoint, held_gradient = (ref.at[i % 2] for ref in held_refs)
         axial_diff, radial_diff, source, spread = [], [], [], []
         for f in range(fields):
@@ -106,6 +103,9 @@
         )
         out = pltpu.make_async_copy(o_ref, out_ref.at[i], out_done)
         out.start()
+        if i + 1 < local:
+            for copy in fetch(i + 1):
+                copy.start()
     out.wait()
 
 

time: 54.2 us -> 53.9 us (level)
  blocking collectives: 24.6 us -> 23.9 us
  Pallas kernels: 8.16 us -> 8.85 us
    pallas_call x5, Pallas kernels: 8.16 us -> 8.85 us  [run(): pl.pallas_call(kernel, out_shape=shapes if len(shapes) > 1 else shapes[0]...]
    all_to_all x1, blocking collectives: 24.6 us -> 23.9 us  [exchange(): lax.all_to_all(x, 'inst', 0, 0, axis_index_groups=[order])]
    all_to_all x1, waiting for transfers between devices: 0.62 us -> 0.01 us  [exchange(): lax.all_to_all(x, 'inst', 0, 0, axis_index_groups=[order])]
where the time goes in v6:
time: 53.9 us; the launch traced here: 53.4 us
  blocking collectives  23.9 us (44%)
  starting transfers between devices  15.5 us (29%)
  Pallas kernels  8.85 us (16%)
  waiting for transfers between devices  5.03 us (9%)
    all_to_all x1, blocking collectives, exchange(): lax.all_to_all(x, 'inst', 0, 0, axis_index_groups=[order])  23.9 us
    all_to_all x1, starting transfers between devices, exchange(): lax.all_to_all(x, 'inst', 0, 0, axis_index_groups=[order])  11.1 us
    pallas_call x5, Pallas kernels, run(): pl.pallas_call(kernel, out_shape=shapes if len(shapes) > 1 else shapes[0]...  8.85 us
    ppermute x1, waiting for transfers between devices, per_device(): lax.ppermute(edges[half:], 'space', up)  4.89 us
    ppermute x1, starting transfers between devices, per_device(): lax.ppermute(edges[half:], 'space', up)  2.4 us
    ppermute x1, starting transfers between devices, per_device(): lax.ppermute(edges[:half], 'space', down)  2.05 us
  transfers between devices with their start and end apart: 3, of which 2 were waited for; matrix products, arithmetic and copies ran while one was open for 0% of the time, Pallas kernels for 0%

profile of v6, /device:TPU:16, one launch (start us, length us, event | category | flops | bytes accessed | tf_op | source)
XLA Modules:
  0.0 53.4 jit_solution(16929832031916890539)
XLA Ops:
  0.0 6.5 %pack.1 = (f32[1280,128]{1,0:T(8,128)S(1)}, f32[160,128]{1,0:T(8,128)S(1)}, f32[4,5,16,512]{3,2,1,0:T(8,128)}) custom-call(s32[1]{0:T(128)} %bitcast.r_0_.me_ref, f32[20,64,128]{2,1,0:T(8,128)} %bitcast.29, s32[8,8,128]{2,1,0:T(8,128)} %bitcast.30, f32[4,5,16,512]{3,2,1,0:T(8,128)} %state_ref.3, f32[4,5,16,512]{3,2,1,0:T(8,128)} %adjoint_ref.1, ...), custom_call_target="tpu_custom_call" | custom-call | bytes 4079620 | tf_op jit(solution)/shard_map/pack/pallas_call | solution.py:256
  6.5 0.0 copy-start.2
  6.5 23.9 %all_to_all.10 = f32[64,5,4,128]{3,2,1,0:T(4,128)S(1)} all-to-all(f32[64,5,4,128]{3,2,1,0:T(4,128)S(1)} %bitcast.28), channel_id=1, replica_groups={{188,192,196,200,204,208,212,216,220,224,228,232,236,240,244,248,252,0,..., dimensions={0} | all-to-all | bytes 1310720 | tf_op jit(solution)/shard_map/all_to_all | solution.py:271
  30.4 0.0 copy-done.2
  30.4 1.3 %time_product.1 = f32[1280,128]{1,0:T(8,128)} custom-call(bf16[256,768]{1,0:T(8,128)(2,1)S(1)} %copy-done.2, f32[1280,128]{1,0:T(8,128)S(1)} %bitcast.26), custom_call_target="tpu_custom_call" | custom-call | flops 251658240 | bytes 2097152 | tf_op jit(solution)/shard_map/time_product/pallas_call | solution.py:256
  31.7 11.1 %all-to-all-start.1 = ((f32[64,5,4,128]{3,2,1,0:T(4,128)}), f32[64,5,4,128]{3,2,1,0:T(4,128)S(1)}, u32[]{:S(2)}, u32[]{:S(2)}) async-start(f32[64,5,4,128]{3,2,1,0:T(4,128)} %bitcast.9), calls=%async_computation.1 | async-start | bytes 1310720 | tf_op jit(solution)/shard_map/all_to_all | solution.py:271
  42.8 0.0 copy-start
  42.8 0.1 interior.1
  42.9 0.0 copy-start.1
  42.9 2.1 %collective-permute-start.1 = (f32[80,128]{1,0:T(8,128)S(1)}, f32[80,128]{1,0:T(8,128)S(1)}, u32[]{:S(2)}, u32[]{:S(2)}) collective-permute-start(f32[80,128]{1,0:T(8,128)S(1)} %get-tuple-element.15), channel_id=1, source_target_pairs={{1,0},{2,1},{3,2},{5,4},{6,5},{7,6},{9,8},{10,9},{11,10},{13,12},{... | collective-permute-start | bytes 122888 | tf_op jit(solution)/shard_map/ppermute | solution.py:348
  45.0 2.4 %collective-permute-start = (f32[80,128]{1,0:T(8,128)S(1)}, f32[80,128]{1,0:T(8,128)S(1)}, u32[]{:S(2)}, u32[]{:S(2)}) collective-permute-start(f32[80,128]{1,0:T(8,128)S(1)} %get-tuple-element.16), channel_id=1, source_target_pairs={{0,1},{1,2},{2,3},{4,5},{5,6},{6,7},{8,9},{9,10},{10,11},{12,13},{... | collective-permute-start | bytes 122888 | tf_op jit(solution)/shard_map/ppermute | solution.py:347
  47.4 0.1 collective-permute-done.1.after_ref
  47.5 4.9 %collective-permute-done.before_ref = f32[80,128]{1,0:T(8,128)S(1)} collective-permute-done((f32[80,128]{1,0:T(8,128)S(1)}, f32[80,128]{1,0:T(8,128)S(1)}, u32[]{:S(2)}, u32[]{:S(2)}) %collective-permute-start) | collective-permute-done | bytes 40992 | tf_op jit(solution)/shard_map/ppermute | solution.py:347
  52.4 0.0 copy-done
  52.4 0.1 border.1.r_2_
  52.5 0.0 all-to-all-done.1
  52.5 0.0 copy-done.1
  52.5 0.9 %combine.1 = f32[1280,128]{1,0:T(8,128)} custom-call(f32[1280,128]{1,0:T(8,128)S(1)} %bitcast.25, f32[1280,128]{1,0:T(8,128)S(1)} %bitcast.27, f32[2,20,4,128]{3,2,1,0:T(4,128)S(1)} %border.1.r_2_), custom_call_target="tpu_custom_call" | custom-call | bytes 2048000 | tf_op jit(solution)/shard_map/combine/pallas_call | solution.py:256
  (1 shorter events, 0.0 us)
Async XLA Ops:
  6.5 23.9 %copy-start.2 = (bf16[256,768]{1,0:T(8,128)(2,1)S(1)}, bf16[256,768]{1,0:T(8,128)(2,1)}, u32[]{:S(2)}) copy-start(bf16[256,768]{1,0:T(8,128)(2,1)} %constant.6.clone.r_0_) | copy-start | bytes 1179652
  31.7 20.8 %all-to-all-start.1 = ((f32[64,5,4,128]{3,2,1,0:T(4,128)}), f32[64,5,4,128]{3,2,1,0:T(4,128)S(1)}, u32[]{:S(2)}, u32[]{:S(2)}) async-start(f32[64,5,4,128]{3,2,1,0:T(4,128)} %bitcast.9), calls=%async_computation.1 | async-start | bytes 1310720 | tf_op jit(solution)/shard_map/all_to_all | solution.py:271
  42.8 9.6 %copy-start = (f32[4,5,16,512]{3,2,1,0:T(8,128)S(1)}, f32[4,5,16,512]{3,2,1,0:T(8,128)}, u32[]{:S(2)}) copy-start(f32[4,5,16,512]{3,2,1,0:T(8,128)} %state_ref.3) | copy-start | bytes 1966084
  42.9 9.6 %copy-start.1 = (f32[4,5,16,512]{3,2,1,0:T(8,128)S(1)}, f32[4,5,16,512]{3,2,1,0:T(8,128)}, u32[]{:S(2)}) copy-start(f32[4,5,16,512]{3,2,1,0:T(8,128)} %get-tuple-element.13) | copy-start | bytes 1966084
  42.9 4.6 %collective-permute-start.1 = (f32[80,128]{1,0:T(8,128)S(1)}, f32[80,128]{1,0:T(8,128)S(1)}, u32[]{:S(2)}, u32[]{:S(2)}) collective-permute-start(f32[80,128]{1,0:T(8,128)S(1)} %get-tuple-element.15), channel_id=1, source_target_pairs={{1,0},{2,1},{3,2},{5,4},{6,5},{7,6},{9,8},{10,9},{11,10},{13,12},{... | collective-permute-start | bytes 122888 | tf_op jit(solution)/shard_map/ppermute | solution.py:348
  45.0 7.4 %collective-permute-start = (f32[80,128]{1,0:T(8,128)S(1)}, f32[80,128]{1,0:T(8,128)S(1)}, u32[]{:S(2)}, u32[]{:S(2)}) collective-permute-start(f32[80,128]{1,0:T(8,128)S(1)} %get-tuple-element.16), channel_id=1, source_target_pairs={{0,1},{1,2},{2,3},{4,5},{5,6},{6,7},{8,9},{9,10},{10,11},{12,13},{... | collective-permute-start | bytes 122888 | tf_op jit(solution)/shard_map/ppermute | solution.py:347
